TPU v7x, 32 devices: a whole 2x2x4 slice. The times are simulated.
32 devices in a mesh: clip: 8 (over z, x), chan: 4 (over y, core).
Axes of the slice: x: 2, y: 2, z: 4, core: 2. Of those that a mesh axis runs over, the one named last changes fastest.
Arguments:
- clip_input: bfloat16 [8, 16, 7, 7, 2048], P('clip'), may hold values from -6 to 6
- seg_count: int32 [8], P('clip'), may hold values from 8 to 16, as said below
- proj_in_master: float32 [2, 2048, 512], P(None, 'clip', 'chan'), may hold values from -0.125 to 0.125
- conv_master: float32 [2, 3, 3, 512, 512], P(None, None, None, 'clip', 'chan'), may hold values from -0.09375 to 0.09375
- proj_out_master: float32 [2, 512, 2048], P(None, 'chan', 'clip'), may hold values from -0.25 to 0.25
- head_master: float32 [2048, 174], P('clip'), may hold values from -0.5 to 0.5
- gain_first: float32 [2, 512], P(None, 'chan'), may hold values from 0.5 to 1.5
- shift_first: float32 [2, 512], P(None, 'chan'), may hold values from -3 to 3
- taps_near: float32 [2, 3, 3, 512], P(None, None, None, 'chan'), may hold values from -2 to 2
- taps_far: float32 [2, 3, 3, 512], P(None, None, None, 'chan'), may hold values from -2 to 2
- gain_second: float32 [2, 512], P(None, 'chan'), may hold values from 0.5 to 1.5
- shift_second: float32 [2, 512], P(None, 'chan'), may hold values from -3 to 3
- gain_third: float32 [2, 2048], P(None, 'chan'), may hold values from 0.5 to 1.5
- shift_third: float32 [2, 2048], P(None, 'chan'), may hold values from -3 to 3
- head_bias: float32 [174], replicated, may hold values from -3 to 3
- logit_grad: float32 [8, 174], P('clip'), may hold values from -6 to 6
Outputs:
- logits: float32 [8, 174], P('clip')
- input_grad: bfloat16 [8, 16, 7, 7, 2048], P('clip', None, None, None, 'chan')
- proj_in_grad: float32 [2, 2048, 512], P(None, 'clip', 'chan')
- conv_grad: float32 [2, 3, 3, 512, 512], P(None, None, None, 'clip', 'chan')
- proj_out_grad: float32 [2, 512, 2048], P(None, 'chan', 'clip')
- head_grad: float32 [2048, 174], P('clip')
- gain_first_grad: float32 [2, 512], P(None, 'chan')
- shift_first_grad: float32 [2, 512], P(None, 'chan')
- taps_near_grad: float32 [2, 3, 3, 512], P(None, None, None, 'chan')
- taps_far_grad: float32 [2, 3, 3, 512], P(None, None, None, 'chan')
- gain_second_grad: float32 [2, 512], P(None, 'chan')
- shift_second_grad: float32 [2, 512], P(None, 'chan')
- gain_third_grad: float32 [2, 2048], P(None, 'chan')
- shift_third_grad: float32 [2, 2048], P(None, 'chan')
- head_bias_grad: float32 [174], replicated
Inputs may be any that keep to these rules, and one draw needn't show every extreme that they name: `seg_count`: each entry is half of 16 or 16; exactly half of the clips hold 16.
All inputs are finite; a program needn't handle non-finite values.
Results may differ from a plain program's by a relative error of at most 0.03.
Values may be sent and summed in bfloat16 or wider, within the bound.
No kernel may reach another device: no remote copies, remote signals or barrier semaphores. Data moves between devices by JAX's collectives and lax.ppermute only.
A program may use at most 128 MiB of HBM per device.

v0:
```python
import jax
import jax.numpy as jnp
from jax import lax
from jax.sharding import PartitionSpec as P

epsilon = 1e-05


def norm_rows(value, valid_mask, gain, shift):
    weight = valid_mask[:, :, None, None, None]
    row_count = jnp.sum(valid_mask) * value.shape[2] * value.shape[3]
    row_mean = jnp.sum(value * weight, axis=(0, 1, 2, 3)) / row_count
    centred = value - row_mean
    variance = jnp.sum(centred * centred * weight, axis=(0, 1, 2, 3)) / row_count
    return centred * lax.rsqrt(variance + epsilon) * gain + shift


def differences(value, valid_mask):
    later = jnp.concatenate([value[:, 1:], jnp.zeros_like(value[:, :1])], axis=1)
    next_valid = jnp.concatenate([valid_mask[:, 1:], jnp.zeros_like(valid_mask[:, :1])], axis=1)
    return (later - value) * next_valid[:, :, None, None, None]


def depthwise(value, kernel, dilation):
    padded = jnp.pad(value, ((0, 0), (0, 0), (dilation, dilation), (dilation, dilation), (0, 0)))
    height = value.shape[2]
    across = value.shape[3]
    result = jnp.zeros_like(value)
    for row_tap in range(3):
        for col_tap in range(3):
            window = padded[
                :,
                :,
                row_tap * dilation : row_tap * dilation + height,
                col_tap * dilation : col_tap * dilation + across,
                :,
            ]
            result = result + window * kernel[row_tap, col_tap]
    return result


def gate_part(first_pre, valid_mask, gain, shift, kernel_near, kernel_far):
    activated = jax.nn.silu(norm_rows(first_pre, valid_mask, gain, shift))
    change = differences(activated, valid_mask)
    gate_logit = depthwise(change, kernel_near, 1) + depthwise(change, kernel_far, 2)
    return activated * (1.0 + jax.nn.sigmoid(gate_logit))


def middle_part(second_pre, valid_mask, gain, shift):
    return jax.nn.silu(norm_rows(second_pre, valid_mask, gain, shift))


def block_part(branch_pre, residual, valid_mask, gain, shift):
    return jax.nn.silu(residual + norm_rows(branch_pre, valid_mask, gain, shift))


def pool_part(block_out, valid_mask):
    weight = valid_mask[:, :, None, None, None]
    totals = jnp.sum(block_out * weight, axis=(1, 2, 3))
    scale = jnp.sum(valid_mask, axis=1) * block_out.shape[2] * block_out.shape[3]
    return totals / scale[:, None]


def spatial_conv(features, kernel):
    flat = features.reshape((-1,) + features.shape[2:])
    result = lax.conv_general_dilated(
        flat,
        kernel,
        (1, 1),
        "SAME",
        dimension_numbers=("NHWC", "HWIO", "NHWC"),
        preferred_element_type=jnp.float32,
    )
    return result.reshape(features.shape[:2] + result.shape[1:])


def conv_weight_grad(features, grad_low):
    height = features.shape[2]
    across = features.shape[3]
    padded = jnp.pad(features, ((0, 0), (0, 0), (1, 1), (1, 1), (0, 0)))
    rows_out = []
    for row_tap in range(3):
        cols_out = []
        for col_tap in range(3):
            window = padded[:, :, row_tap : row_tap + height, col_tap : col_tap + across, :]
            cols_out.append(
                jnp.einsum("nsabi,nsabo->io", window, grad_low, preferred_element_type=jnp.float32)
            )
        rows_out.append(jnp.stack(cols_out, axis=0))
    return jnp.stack(rows_out, axis=0)


def local(
    clip_input,
    seg_count,
    proj_in_master,
    conv_master,
    proj_out_master,
    head_master,
    gain_first,
    shift_first,
    taps_near,
    taps_far,
    gain_second,
    shift_second,
    gain_third,
    shift_third,
    head_bias,
    logit_grad,
):
    chan_index = lax.axis_index("chan")
    layers = proj_in_master.shape[0]
    own_width = gain_third.shape[1]
    valid_mask = (
        jnp.arange(clip_input.shape[1], dtype=jnp.int32)[None, :] < seg_count[:, None]
    ).astype(jnp.float32)
    weight_in, weight_mid, weight_out, weight_head = (
        lax.all_gather(proj_in_master.astype(jnp.bfloat16), "clip", axis=1, tiled=True),
        lax.all_gather(conv_master.astype(jnp.bfloat16), "clip", axis=3, tiled=True),
        lax.all_gather(proj_out_master.astype(jnp.bfloat16), "clip", axis=2, tiled=True),
        lax.all_gather(head_master.astype(jnp.bfloat16), "clip", axis=0, tiled=True),
    )

    def gate_local(pre_value, gain, shift, kernel_near, kernel_far):
        return gate_part(pre_value, valid_mask, gain, shift, kernel_near, kernel_far)

    def middle_local(pre_value, gain, shift):
        return middle_part(pre_value, valid_mask, gain, shift)

    def block_local(pre_value, skip_value, gain, shift):
        return block_part(pre_value, skip_value, valid_mask, gain, shift)

    def pool_local(value):
        return pool_part(value, valid_mask)

    layer_low = clip_input
    residual = lax.dynamic_slice_in_dim(clip_input, chan_index * own_width, own_width, 4).astype(
        jnp.float32
    )
    block_out = residual
    saved = []
    for layer in range(layers):
        if layer > 0:
            next_low = block_out.astype(jnp.bfloat16)
            layer_low = lax.all_gather(next_low, "chan", axis=4, tiled=True)
            residual = next_low.astype(jnp.float32)
        first_pre = jnp.einsum(
            "nsabc,cd->nsabd", layer_low, weight_in[layer], preferred_element_type=jnp.float32
        )
        gated, gate_back = jax.vjp(
            gate_local,
            first_pre,
            gain_first[layer],
            shift_first[layer],
            taps_near[layer],
            taps_far[layer],
        )
        gated_low = gated.astype(jnp.bfloat16)
        gated_all = lax.all_gather(gated_low, "chan", axis=4, tiled=True)
        second_pre = spatial_conv(gated_all, weight_mid[layer])
        second_act, middle_back = jax.vjp(
            middle_local, second_pre, gain_second[layer], shift_second[layer]
        )
        second_low = second_act.astype(jnp.bfloat16)
        branch_part = jnp.einsum(
            "nsabc,cd->nsabd", second_low, weight_out[layer], preferred_element_type=jnp.float32
        )
        branch_pre = lax.psum_scatter(
            branch_part.astype(jnp.bfloat16), "chan", scatter_dimension=4, tiled=True
        ).astype(jnp.float32)
        block_out, top_back = jax.vjp(
            block_local, branch_pre, residual, gain_third[layer], shift_third[layer]
        )
        inner_kept = gated_all
        saved.append((layer_low, gate_back, inner_kept, middle_back, second_low, top_back))
    pooled, pool_back = jax.vjp(pool_local, block_out)
    pooled_all = lax.all_gather(pooled.astype(jnp.bfloat16), "chan", axis=1, tiled=True)
    logits = jnp.dot(pooled_all, weight_head, preferred_element_type=jnp.float32) + head_bias
    grad_low = logit_grad.astype(jnp.bfloat16)
    bias_grad = jnp.sum(grad_low.astype(jnp.float32), axis=0)
    head_term = jnp.dot(pooled_all.T, grad_low, preferred_element_type=jnp.float32)
    head_own = lax.dynamic_slice_in_dim(weight_head, chan_index * own_width, own_width, 0)
    pooled_grad = jnp.dot(grad_low, head_own.T, preferred_element_type=jnp.float32)
    out_cot = pool_back(pooled_grad)[0]
    in_terms = [None] * layers
    mid_terms = [None] * layers
    out_terms = [None] * layers
    small_terms = [None] * layers
    for layer in reversed(range(layers)):
        layer_low, gate_back, inner_kept, middle_back, second_low, top_back = saved[layer]
        branch_grad, residual_grad, gain_three_grad, shift_three_grad = top_back(out_cot)
        branch_low = branch_grad.astype(jnp.bfloat16)
        branch_all = lax.all_gather(branch_low, "chan", axis=4, tiled=True)
        second_act_grad = jnp.einsum(
            "nsabd,cd->nsabc", branch_all, weight_out[layer], preferred_element_type=jnp.float32
        )
        out_terms[layer] = jnp.einsum(
            "nsabc,nsabd->cd", second_low, branch_all, preferred_element_type=jnp.float32
        )
        second_grad, gain_two_grad, shift_two_grad = middle_back(second_act_grad)
        second_grad_low = second_grad.astype(jnp.bfloat16)
        mid_terms[layer] = conv_weight_grad(inner_kept, second_grad_low)
        flipped = jnp.transpose(jnp.flip(weight_mid[layer], (0, 1)), (0, 1, 3, 2))
        gated_part = spatial_conv(second_grad_low, flipped)
        gated_grad = lax.psum_scatter(
            gated_part.astype(jnp.bfloat16), "chan", scatter_dimension=4, tiled=True
        ).astype(jnp.float32)
        first_grad, gain_one_grad, shift_one_grad, near_grad, far_grad = gate_back(gated_grad)
        first_low = first_grad.astype(jnp.bfloat16)
        in_terms[layer] = jnp.einsum(
            "nsabc,nsabd->cd", layer_low, first_low, preferred_element_type=jnp.float32
        )
        input_part = jnp.einsum(
            "nsabd,cd->nsabc", first_low, weight_in[layer], preferred_element_type=jnp.float32
        )
        input_sum = lax.psum_scatter(
            input_part.astype(jnp.bfloat16), "chan", scatter_dimension=4, tiled=True
        ).astype(jnp.float32)
        out_cot = input_sum + residual_grad
        small_terms[layer] = (
            gain_one_grad,
            shift_one_grad,
            near_grad,
            far_grad,
            gain_two_grad,
            shift_two_grad,
            gain_three_grad,
            shift_three_grad,
        )
    input_grad = out_cot.astype(jnp.bfloat16)
    in_share, mid_share, out_share, head_share = (
        lax.psum_scatter(jnp.stack(in_terms), "clip", scatter_dimension=1, tiled=True),
        lax.psum_scatter(jnp.stack(mid_terms), "clip", scatter_dimension=3, tiled=True),
        lax.psum_scatter(jnp.stack(out_terms), "clip", scatter_dimension=2, tiled=True),
        lax.psum_scatter(head_term, "clip", scatter_dimension=0, tiled=True),
    )
    stacked = tuple(
        (jnp.stack([small_terms[layer][member] for layer in range(layers)]) for member in range(8))
    )
    summed = lax.psum(
        (
            stacked[0],
            stacked[1],
            stacked[2],
            stacked[3],
            stacked[4],
            stacked[5],
            stacked[6],
            stacked[7],
            bias_grad,
        ),
        "clip",
    )
    return (
        logits,
        input_grad,
        in_share,
        mid_share,
        out_share,
        head_share,
        summed[0],
        summed[1],
        summed[2],
        summed[3],
        summed[4],
        summed[5],
        summed[6],
        summed[7],
        summed[8],
    )


def solution(mesh):
    in_specs = (
        P("clip", None, None, None, None),
        P("clip"),
        P(None, "clip", "chan"),
        P(None, None, None, "clip", "chan"),
        P(None, "chan", "clip"),
        P("clip", None),
        P(None, "chan"),
        P(None, "chan"),
        P(None, None, None, "chan"),
        P(None, None, None, "chan"),
        P(None, "chan"),
        P(None, "chan"),
        P(None, "chan"),
        P(None, "chan"),
        P(),
        P("clip", None),
    )
    out_specs = (
        P("clip", None),
        P("clip", None, None, None, "chan"),
        P(None, "clip", "chan"),
        P(None, None, None, "clip", "chan"),
        P(None, "chan", "clip"),
        P("clip", None),
        P(None, "chan"),
        P(None, "chan"),
        P(None, None, None, "chan"),
        P(None, None, None, "chan"),
        P(None, "chan"),
        P(None, "chan"),
        P(None, "chan"),
        P(None, "chan"),
        P(),
    )
    return jax.shard_map(local, mesh=mesh, in_specs=in_specs, out_specs=out_specs, check_vma=False)
```

profile of v0, /device:TPU:8, one launch (start us, length us, event | category | flops | bytes accessed | tf_op | source)
XLA Modules:
  0.0 864.2 jit_solution(12466073082788043999)
XLA Ops:
  7.3 1.7 convert_element_type.157
  9.1 1.8 convert_element_type.161
  14.0 37.2 %all-gather.9.cloned.1.call-done = bf16[2,2048,128]{2,1,0:T(8,128)(2,1)} async-done(((bf16[2,256,128]{2,1,0:T(8,128)(2,1)}), bf16[2,2048,128]{2,1,0:T(8,128)(2,1)}) %all-gather.9.cloned.1.call-update) | async-done | bytes 1048592 | tf_op jit(solution)/shard_map/all_gather | solution.py:118
  51.3 3.0 multiply_reduce_fusion.46
  57.5 8.7 %all_gather.31 = bf16[1,16,7,7,512]{4,1,3,2,0:T(8,128)(2,1)S(1)} all-gather(bf16[1,16,7,7,128]{4,1,3,2,0:T(8,128)(2,1)S(1)} %get-tuple-element.144), channel_id=1, replica_groups=mesh['clip'=8,'chan'=4] {'chan'}, dimensions={4}, use_global_device_ids=true | all-gather | bytes 1003520 | tf_op jit(solution)/shard_map/all_gather | solution.py:159
  66.2 39.5 %all-gather.11.cloned.1.call-done = bf16[2,3,3,512,128]{4,3,2,1,0:T(8,128)(2,1)} async-done(((bf16[2,3,3,64,128]{4,3,2,1,0:T(8,128)(2,1)}), bf16[2,3,3,512,128]{4,3,2,1,0:T(8,128)(2,1)}) %all-gather.11.cloned.1.call-update) | async-done | bytes 2359312 | tf_op jit(solution)/shard_map/all_gather | solution.py:119
  105.7 3.3 multiply_reduce_fusion.44
  109.7 36.0 %all-gather.13.cloned.1.call-done = bf16[2,128,2048]{2,1,0:T(8,128)(2,1)} async-done(((bf16[2,128,256]{2,1,0:T(8,128)(2,1)}), bf16[2,128,2048]{2,1,0:T(8,128)(2,1)}) %all-gather.13.cloned.1.call-update) | async-done | bytes 1048592 | tf_op jit(solution)/shard_map/all_gather | solution.py:120
  145.8 3.8 fusion.16
  150.2 37.4 %reduce-scatter.15.cloned.1.call-done = bf16[1,16,7,7,512]{4,1,3,2,0:T(8,128)(2,1)} async-done(((bf16[1,16,7,7,2048]{4,1,3,2,0:T(8,128)(2,1)}), bf16[1,16,7,7,512]{4,1,3,2,0:T(8,128)(2,1)}) %reduce-scatter.15.cloned.1.call-update) | async-done | bytes 802832 | tf_op jit(solution)/shard_map/reduce_scatter | solution.py:168
  187.6 1.6 fusion.53
  190.7 2.8 multiply_convert_fusion
  193.7 28.8 %all-gather.15.cloned.1.call-done = bf16[1,16,7,7,2048]{4,1,3,2,0:T(8,128)(2,1)} async-done(((bf16[1,16,7,7,512]{4,1,3,2,0:T(8,128)(2,1)}), bf16[1,16,7,7,2048]{4,1,3,2,0:T(8,128)(2,1)}) %all-gather.15.cloned.1.call-update) | async-done | bytes 3211280 | tf_op jit(solution)/shard_map/all_gather | solution.py:145
  222.6 2.9 multiply_reduce_fusion.42
  228.2 8.7 %all_gather.35 = bf16[1,16,7,7,512]{4,1,3,2,0:T(8,128)(2,1)S(1)} all-gather(bf16[1,16,7,7,128]{4,1,3,2,0:T(8,128)(2,1)S(1)} %get-tuple-element.138), channel_id=1, replica_groups=mesh['clip'=8,'chan'=4] {'chan'}, dimensions={4}, use_global_device_ids=true | all-gather | bytes 1003520 | tf_op jit(solution)/shard_map/all_gather | solution.py:159
  236.9 2.0 multiply_reduce_fusion.40
  239.7 2.7 fusion.17
  243.4 29.7 %all_gather.37 = bf16[2048,174]{0,1:T(8,128)(2,1)S(1)} all-gather(bf16[256,174]{0,1:T(8,128)(2,1)S(1)} %convert_element_type.176), channel_id=1, replica_groups=mesh['clip'=8,'chan'=4] {'clip'}, dimensions={0}, use_global_device_ids=true | all-gather | bytes 801792 | tf_op jit(solution)/shard_map/all_gather | solution.py:121
  274.1 6.9 reduce-scatter.17.cloned.1.call-done
  288.0 29.0 %all-gather.17.cloned.1.call-done = bf16[1,16,7,7,2048]{4,1,3,2,0:T(8,128)(2,1)} async-done(((bf16[1,16,7,7,512]{4,1,3,2,0:T(8,128)(2,1)}), bf16[1,16,7,7,2048]{4,1,3,2,0:T(8,128)(2,1)}) %all-gather.17.cloned.1.call-update) | async-done | bytes 3211280 | tf_op jit(solution)/shard_map/all_gather | solution.py:193
  316.9 3.7 fusion.187
  322.8 7.2 copy.70
  329.9 8.5 reshape.1015
  338.7 24.0 %reduce-scatter.31.cloned.1.call-done = bf16[128,784]{1,0:T(8,128)(2,1)} async-done(((bf16[512,784]{1,0:T(8,128)(2,1)}), bf16[128,784]{1,0:T(8,128)(2,1)}) %reduce-scatter.31.cloned.1.call-update) | async-done | bytes 200720
  362.6 3.3 reshape.1016
  366.1 3.3 copy.71
  373.1 2.7 fusion.18
  375.9 38.4 %reduce-scatter.19.cloned.1.call-done = bf16[1,16,7,7,512]{4,1,3,2,0:T(8,128)(2,1)} async-done(((bf16[1,16,7,7,2048]{4,1,3,2,0:T(8,128)(2,1)}), bf16[1,16,7,7,512]{4,1,3,2,0:T(8,128)(2,1)}) %reduce-scatter.19.cloned.1.call-update) | async-done | bytes 802832 | tf_op jit(solution)/shard_map/reduce_scatter | solution.py:216
  414.3 3.1 fusion.184
  419.5 29.0 %all-gather.19.cloned.1.call-done = bf16[1,16,7,7,2048]{4,1,3,2,0:T(8,128)(2,1)} async-done(((bf16[1,16,7,7,512]{4,1,3,2,0:T(8,128)(2,1)}), bf16[1,16,7,7,2048]{4,1,3,2,0:T(8,128)(2,1)}) %all-gather.19.cloned.1.call-update) | async-done | bytes 3211280 | tf_op jit(solution)/shard_map/all_gather | solution.py:193
  448.6 3.7 fusion.186
  454.4 7.2 copy.72
  461.6 8.5 reshape.1017
  470.4 3.8 fusion.23
  474.2 20.2 %reduce-scatter.33.cloned.1.call-done = bf16[128,784]{1,0:T(8,128)(2,1)} async-done(((bf16[512,784]{1,0:T(8,128)(2,1)}), bf16[128,784]{1,0:T(8,128)(2,1)}) %reduce-scatter.33.cloned.1.call-update) | async-done | bytes 200720
  494.4 3.3 reshape.1018
  497.8 3.3 copy.73
  508.3 3.8 fusion.19
  512.8 5.2 all-gather.1
  533.0 1.7 convolution_bitcast_fusion.7
  540.8 2.6 pad_maximum_fusion
  546.6 34.9 %all-reduce.80 = (f32[2,128]{1,0:T(2,128)}, f32[2,128]{1,0:T(2,128)}, f32[2,3,3,128]{3,2,1,0:T(4,128)S(1)}, f32[2,3,3,128]{3,2,1,0:T(4,128)S(1)}, f32[2,128]{1,0...) all-reduce(f32[2,128]{1,0:T(2,128)S(1)} %pad_maximum_fusion.7, ...), channel_id=1, replica_groups=mesh['clip'=8,'chan'=4] {'clip'}, use_global_device_ids=true, to_apply=%region_38.39 | all-reduce | flops 7854 | bytes 62484 | tf_op jit(solution)/shard_map/psum | solution.py:240
  582.8 1.8 copy.40
  584.6 32.5 %reduce-scatter.21.cloned.1.call-done = bf16[1,16,7,7,512]{4,1,3,2,0:T(8,128)(2,1)} async-done(((bf16[1,16,7,7,2048]{4,1,3,2,0:T(8,128)(2,1)}), bf16[1,16,7,7,512]{4,1,3,2,0:T(8,128)(2,1)}) %reduce-scatter.21.cloned.1.call-update) | async-done | bytes 802832 | tf_op jit(solution)/shard_map/reduce_scatter | solution.py:216
  617.1 2.3 add_convert_fusion
  619.4 67.4 %reduce-scatter.29.cloned.1.call-done = f32[256,174]{0,1:T(8,128)} async-done(((f32[2048,174]{0,1:T(8,128)}), f32[256,174]{0,1:T(8,128)}) %reduce-scatter.29.cloned.1.call-update) | async-done | bytes 178192 | tf_op jit(solution)/shard_map/reduce_scatter | solution.py:235
  686.8 70.9 %reduce-scatter.27.cloned.1.call-done = f32[2,128,256]{2,1,0:T(8,128)} async-done(((f32[2,128,2048]{2,1,0:T(8,128)}), f32[2,128,256]{2,1,0:T(8,128)}) %reduce-scatter.27.cloned.1.call-update) | async-done | bytes 262160 | tf_op jit(solution)/shard_map/reduce_scatter | solution.py:234
  757.7 99.6 %reduce-scatter.25.cloned.1.call-done = f32[2,3,3,64,128]{4,3,2,1,0:T(8,128)} async-done(((f32[2,3,3,512,128]{4,3,2,1,0:T(8,128)}), f32[2,3,3,64,128]{4,3,2,1,0:T(8,128)}) %reduce-scatter.25.cloned.1.call-update) | async-done | bytes 589840 | tf_op jit(solution)/shard_map/reduce_scatter | solution.py:233
  (476 shorter events, 62.9 us)
Async XLA Ops:
  7.3 44.0 %all-gather.9.cloned.1.call-start = ((), (), s32[]{:S(2)}) async-start(), calls=%async_computation.10 | async-start | bytes 1179648 | tf_op jit(solution)/shard_map/all_gather | solution.py:118
  9.0 96.7 %all-gather.11.cloned.1.call-start = ((), (), s32[]{:S(2)}) async-start(), calls=%async_computation.11 | async-start | bytes 2654208 | tf_op jit(solution)/shard_map/all_gather | solution.py:119
  10.9 134.8 %all-gather.13.cloned.1.call-start = ((), (), s32[]{:S(2)}) async-start(), calls=%async_computation.12 | async-start | bytes 1179648 | tf_op jit(solution)/shard_map/all_gather | solution.py:120
  11.7 175.9 %reduce-scatter.15.cloned.1.call-start = ((), (), s32[]{:S(2)}) async-start(), calls=%async_computation.13 | async-start | bytes 4014080 | tf_op jit(solution)/shard_map/reduce_scatter | solution.py:168
  13.1 42.3 %copy-start.39 = (f32[128]{0:T(128)}, f32[128]{0:T(128)S(1)}, u32[]{:S(2)}) copy-start(f32[128]{0:T(128)S(1)} %get-tuple-element.214) | copy-start | bytes 1540
  13.2 42.2 %copy-start.41 = (f32[128]{0:T(128)}, f32[128]{0:T(128)S(1)}, u32[]{:S(2)}) copy-start(f32[128]{0:T(128)S(1)} %get-tuple-element.215) | copy-start | bytes 1540
  13.2 42.2 %copy-start.43 = (f32[128]{0:T(128)}, f32[128]{0:T(128)S(1)}, u32[]{:S(2)}) copy-start(f32[128]{0:T(128)S(1)} %get-tuple-element.216) | copy-start | bytes 1540
  13.2 42.2 %copy-start.45 = (f32[128]{0:T(128)}, f32[128]{0:T(128)S(1)}, u32[]{:S(2)}) copy-start(f32[128]{0:T(128)S(1)} %get-tuple-element.217) | copy-start | bytes 1540
  13.2 42.2 %copy-start.47 = (f32[128]{0:T(128)}, f32[128]{0:T(128)S(1)}, u32[]{:S(2)}) copy-start(f32[128]{0:T(128)S(1)} %get-tuple-element.218) | copy-start | bytes 1540
  13.2 42.2 %copy-start.49 = (f32[128]{0:T(128)}, f32[128]{0:T(128)S(1)}, u32[]{:S(2)}) copy-start(f32[128]{0:T(128)S(1)} %get-tuple-element.219) | copy-start | bytes 1540
  13.2 42.2 %copy-start.51 = (f32[128]{0:T(128)}, f32[128]{0:T(128)S(1)}, u32[]{:S(2)}) copy-start(f32[128]{0:T(128)S(1)} %get-tuple-element.220) | copy-start | bytes 1540
  13.2 42.2 %copy-start.53 = (f32[128]{0:T(128)}, f32[128]{0:T(128)S(1)}, u32[]{:S(2)}) copy-start(f32[128]{0:T(128)S(1)} %get-tuple-element.221) | copy-start | bytes 1540
  13.2 42.2 %copy-start.55 = (f32[128]{0:T(128)}, f32[128]{0:T(128)S(1)}, u32[]{:S(2)}) copy-start(f32[128]{0:T(128)S(1)} %get-tuple-element.222) | copy-start | bytes 1540
  13.2 42.2 %copy-start.57 = (f32[128]{0:T(128)}, f32[128]{0:T(128)S(1)}, u32[]{:S(2)}) copy-start(f32[128]{0:T(128)S(1)} %get-tuple-element.223) | copy-start | bytes 1540
  14.0 131.7 %copy-start.95 = (f32[128]{0:T(128)}, f32[128]{0:T(128)S(1)}, u32[]{:S(2)}) copy-start(f32[128]{0:T(128)S(1)} %get-tuple-element.231) | copy-start | bytes 1540
  14.0 225.7 %copy-start.98 = (f32[128]{0:T(128)}, f32[128]{0:T(128)S(1)}, u32[]{:S(2)}) copy-start(f32[128]{0:T(128)S(1)} %get-tuple-element.230) | copy-start | bytes 1540
  66.2 42.8 %copy-start.21 = (bf16[1,16,7,7,512]{4,1,3,2,0:T(8,128)(2,1)}, bf16[1,16,7,7,512]{4,1,3,2,0:T(8,128)(2,1)S(1)}, u32[]{:S(2)}) copy-start(bf16[1,16,7,7,512]{4,1,3,2,0:T(8,128)(2,1)S(1)} %all_gather.31) | copy-start | bytes 2408452
  149.6 73.0 %all-gather.15.cloned.1.call-start = ((), (), s32[]{:S(2)}) async-start(), calls=%async_computation.14 | async-start | bytes 4014080 | tf_op jit(solution)/shard_map/all_gather | solution.py:145
  193.5 87.5 %reduce-scatter.17.cloned.1.call-start = ((), (), s32[]{:S(2)}) async-start(), calls=%async_computation.15 | async-start | bytes 4014080 | tf_op jit(solution)/shard_map/reduce_scatter | solution.py:168
  193.6 33.1 %copy-start.59 = (f32[128]{0:T(128)}, f32[128]{0:T(128)S(1)}, u32[]{:S(2)}) copy-start(f32[128]{0:T(128)S(1)} %get-tuple-element.190) | copy-start | bytes 1540
  193.6 33.1 %copy-start.61 = (f32[128]{0:T(128)}, f32[128]{0:T(128)S(1)}, u32[]{:S(2)}) copy-start(f32[128]{0:T(128)S(1)} %get-tuple-element.191) | copy-start | bytes 1540
  193.6 33.1 %copy-start.63 = (f32[128]{0:T(128)}, f32[128]{0:T(128)S(1)}, u32[]{:S(2)}) copy-start(f32[128]{0:T(128)S(1)} %get-tuple-element.192) | copy-start | bytes 1540
  193.6 33.1 %copy-start.65 = (f32[128]{0:T(128)}, f32[128]{0:T(128)S(1)}, u32[]{:S(2)}) copy-start(f32[128]{0:T(128)S(1)} %get-tuple-element.193) | copy-start | bytes 1540
  193.6 33.1 %copy-start.67 = (f32[128]{0:T(128)}, f32[128]{0:T(128)S(1)}, u32[]{:S(2)}) copy-start(f32[128]{0:T(128)S(1)} %get-tuple-element.194) | copy-start | bytes 1540
  193.6 33.1 %copy-start.69 = (f32[128]{0:T(128)}, f32[128]{0:T(128)S(1)}, u32[]{:S(2)}) copy-start(f32[128]{0:T(128)S(1)} %get-tuple-element.195) | copy-start | bytes 1540
  193.6 33.1 %copy-start.71 = (f32[128]{0:T(128)}, f32[128]{0:T(128)S(1)}, u32[]{:S(2)}) copy-start(f32[128]{0:T(128)S(1)} %get-tuple-element.196) | copy-start | bytes 1540
  193.6 33.0 %copy-start.73 = (f32[128]{0:T(128)}, f32[128]{0:T(128)S(1)}, u32[]{:S(2)}) copy-start(f32[128]{0:T(128)S(1)} %get-tuple-element.197) | copy-start | bytes 1540
  193.7 33.0 %copy-start.75 = (f32[128]{0:T(128)}, f32[128]{0:T(128)S(1)}, u32[]{:S(2)}) copy-start(f32[128]{0:T(128)S(1)} %get-tuple-element.198) | copy-start | bytes 1540
  193.7 33.0 %copy-start.77 = (f32[128]{0:T(128)}, f32[128]{0:T(128)S(1)}, u32[]{:S(2)}) copy-start(f32[128]{0:T(128)S(1)} %get-tuple-element.199) | copy-start | bytes 1540
  193.7 33.0 %copy-start.79 = (f32[128]{0:T(128)}, f32[128]{0:T(128)S(1)}, u32[]{:S(2)}) copy-start(f32[128]{0:T(128)S(1)} %get-tuple-element.200) | copy-start | bytes 1540
  193.7 33.0 %copy-start.81 = (f32[128]{0:T(128)}, f32[128]{0:T(128)S(1)}, u32[]{:S(2)}) copy-start(f32[128]{0:T(128)S(1)} %get-tuple-element.201) | copy-start | bytes 1540
  193.7 33.0 %copy-start.83 = (f32[128]{0:T(128)}, f32[128]{0:T(128)S(1)}, u32[]{:S(2)}) copy-start(f32[128]{0:T(128)S(1)} %get-tuple-element.202) | copy-start | bytes 1540
  193.7 33.0 %copy-start.85 = (f32[128]{0:T(128)}, f32[128]{0:T(128)S(1)}, u32[]{:S(2)}) copy-start(f32[128]{0:T(128)S(1)} %get-tuple-element.203) | copy-start | bytes 1540
  193.7 33.0 %copy-start.87 = (f32[128]{0:T(128)}, f32[128]{0:T(128)S(1)}, u32[]{:S(2)}) copy-start(f32[128]{0:T(128)S(1)} %get-tuple-element.204) | copy-start | bytes 1540
  193.7 33.0 %copy-start.89 = (f32[128]{0:T(128)}, f32[128]{0:T(128)S(1)}, u32[]{:S(2)}) copy-start(f32[128]{0:T(128)S(1)} %get-tuple-element.205) | copy-start | bytes 1540
  239.0 82.4 %copy-start.5 = (f32[16,7,7,128]{3,0,2,1:T(8,128)}, f32[16,7,7,128]{3,0,2,1:T(8,128)S(1)}, u32[]{:S(2)}) copy-start(f32[16,7,7,128]{3,0,2,1:T(8,128)S(1)} %get-tuple-element.247) | copy-start | bytes 1204228
  242.5 41.6 %copy-start.4 = (bf16[1,16,7,7,512]{4,1,3,2,0:T(8,128)(2,1)S(1)}, bf16[1,16,7,7,512]{4,1,3,2,0:T(8,128)(2,1)}, u32[]{:S(2)}) copy-start(bf16[1,16,7,7,512]{4,1,3,2,0:T(8,128)(2,1)} %multiply_convert_fusion) | copy-start | bytes 2408452
  242.5 74.5 %all-gather.17.cloned.1.call-start = ((), (), s32[]{:S(2)}) async-start(), calls=%async_computation.16 | async-start | bytes 4014080 | tf_op jit(solution)/shard_map/all_gather | solution.py:193
  287.9 74.7 %reduce-scatter.31.cloned.1.call-start = ((), (), s32[]{:S(2)}) async-start(), calls=%async_computation.24 | async-start | bytes 1146880
  338.4 75.9 %reduce-scatter.19.cloned.1.call-start = ((), (), s32[]{:S(2)}) async-start(), calls=%async_computation.17 | async-start | bytes 4014080 | tf_op jit(solution)/shard_map/reduce_scatter | solution.py:216
  375.8 72.7 %all-gather.19.cloned.1.call-start = ((), (), s32[]{:S(2)}) async-start(), calls=%async_computation.18 | async-start | bytes 4014080 | tf_op jit(solution)/shard_map/all_gather | solution.py:193
  419.5 32.8 %copy-start.136 = (f32[128]{0:T(128)S(1)}, f32[128]{0:T(128)}, u32[]{:S(2)}) copy-start(f32[128]{0:T(128)} %get-tuple-element.143) | copy-start | bytes 1540
  419.5 74.9 %reduce-scatter.33.cloned.1.call-start = ((), (), s32[]{:S(2)}) async-start(), calls=%async_computation.25 | async-start | bytes 1146880
  470.1 112.7 %reduce-scatter.23.cloned.1.call-start = ((), (), s32[]{:S(2)}) async-start(), calls=%async_computation.20 | async-start | bytes 2359296 | tf_op jit(solution)/shard_map/reduce_scatter | solution.py:232
  508.2 108.9 %reduce-scatter.21.cloned.1.call-start = ((), (), s32[]{:S(2)}) async-start(), calls=%async_computation.19 | async-start | bytes 4014080 | tf_op jit(solution)/shard_map/reduce_scatter | solution.py:216
  512.1 174.7 %reduce-scatter.29.cloned.1.call-start = ((), (), s32[]{:S(2)}) async-start(), calls=%async_computation.23 | async-start | bytes 1622016 | tf_op jit(solution)/shard_map/reduce_scatter | solution.py:235
  519.4 238.3 %reduce-scatter.27.cloned.1.call-start = ((), (), s32[]{:S(2)}) async-start(), calls=%async_computation.22 | async-start | bytes 2359296 | tf_op jit(solution)/shard_map/reduce_scatter | solution.py:234
  531.0 326.3 %reduce-scatter.25.cloned.1.call-start = ((), (), s32[]{:S(2)}) async-start(), calls=%async_computation.21 | async-start | bytes 5308416 | tf_op jit(solution)/shard_map/reduce_scatter | solution.py:233
  (121 other events, 645.7 us)
Sparse Core Ops, SparseCore 0:
  10.8 40.3 all-gather.8
  54.0 51.6 all-gather.10
  108.3 37.3 all-gather.12
  149.7 37.8 reduce-scatter.14
  193.6 28.9 all-gather.14
  242.6 38.3 reduce-scatter.16
  288.0 28.8 all-gather.16
  338.5 24.0 reduce-scatter.30
  376.0 38.3 reduce-scatter.18
  419.6 28.9 all-gather.18
  470.3 24.0 reduce-scatter.32
  508.3 67.8 reduce-scatter.22
  578.9 38.1 reduce-scatter.20
  621.0 65.7 reduce-scatter.28
  690.8 66.8 reduce-scatter.26
  761.8 95.4 reduce-scatter.24
where the time goes:
time: 875 us; the launch traced here: 864 us
  waiting for transfers between devices  597 us (68%)
  blocking collectives  87.2 us (10%)
  local copies, waits for them, and re-layouts  58.9 us (7%)
  matrix products  52.2 us (6%)
  other arithmetic  49.5 us (6%)
  between operations  18 us (2%)
    reduce_scatter x1, waiting for transfers between devices, local(): lax.psum_scatter(jnp.stack(mid_terms), 'clip', scatter_dimension=3, tiled...  99.6 us
    reduce_scatter x2, waiting for transfers between devices, local(): lax.psum_scatter(input_part.astype(jnp.bfloat16), 'chan', scatter_dimensi...  70.9 us
    reduce_scatter x1, waiting for transfers between devices, local(): lax.psum_scatter(jnp.stack(out_terms), 'clip', scatter_dimension=2, tiled...  70.9 us
    reduce_scatter x1, waiting for transfers between devices, local(): lax.psum_scatter(head_term, 'clip', scatter_dimension=0, tiled=True)  67.4 us
    unnamed x321, local copies, waits for them, and re-layouts  58.7 us
    all_gather x2, waiting for transfers between devices, local(): branch_all = lax.all_gather(branch_low, 'chan', axis=4, tiled=True)  58 us
    unnamed x18, waiting for transfers between devices  44.4 us
    reduce_scatter x2, waiting for transfers between devices, local(): lax.psum_scatter(branch_part.astype(jnp.bfloat16), 'chan', scatter_dimens...  44.3 us
  transfers between devices with their start and end apart: 16, of which 15 were waited for; matrix products, arithmetic and copies ran while one was open for 6% of the time, Pallas kernels for 0%

commit v1 on v0

v1 whole, which is shorter than its diff:
```python
import types

import jax
import jax.numpy as jnp
from jax import lax
from jax.experimental import pallas as pl
from jax.experimental.pallas import tpu as pltpu
from jax.sharding import PartitionSpec as P

EPS = 1e-05
LANE = 128
WPAD = 8
CHUNK = 256
bf16 = jnp.bfloat16
f32 = jnp.float32


def call(name, body, ins, outs, scratch, flops=0, nbytes=0, limit=60):
    in_names, out_names, scratch_names = list(ins), list(outs), list(scratch)

    def kernel(*refs):
        body(types.SimpleNamespace(**dict(zip(in_names + out_names + scratch_names, refs))))

    results = pl.pallas_call(
        kernel,
        name=name,
        out_shape=[jax.ShapeDtypeStruct(*outs[n]) for n in out_names],
        in_specs=[pl.BlockSpec(memory_space=ins[n][1]) for n in in_names],
        out_specs=[pl.BlockSpec(memory_space=pltpu.VMEM) for _ in out_names],
        scratch_shapes=[scratch[n] for n in scratch_names],
        compiler_params=pltpu.CompilerParams(vmem_limit_bytes=limit * 1024 * 1024),
        cost_estimate=pl.CostEstimate(flops=flops, bytes_accessed=nbytes, transcendentals=0),
    )(*[ins[n][0] for n in in_names])
    return dict(zip(out_names, results))


VM = pltpu.VMEM
SM = pltpu.SMEM
HB = pl.ANY
COUNT, OWN, ORDER = 0, 1, 2


def lanes(start, size=LANE):
    return pl.ds(pl.multiple_of(start, LANE), size)


def dot(a, b):
    return jnp.dot(a, b, preferred_element_type=f32)


def dot_nt(a, b):
    return lax.dot_general(a, b, (((1,), (1,)), ((), ())), preferred_element_type=f32)


def sigmoid(v):
    return 1.0 / (1.0 + jnp.exp(-v))


def rotate(v, k):
    if k == 0:
        return v
    groups = v.reshape(v.shape[0] // WPAD, WPAD, v.shape[1])
    return pltpu.roll(groups, (-k) % WPAD, axis=1).reshape(v.shape)


class Geometry:
    def __init__(self, seg, high, wide):
        self.seg, self.high, self.wide = seg, high, wide
        self.step = seg * WPAD
        self.rows = high * self.step

    def block(self, h):
        return slice(h * self.step, (h + 1) * self.step)


def fill_masks(r, geo):
    count = r.meta[COUNT]
    row = lax.broadcasted_iota(jnp.int32, (geo.step, LANE), 0)
    seg = row // WPAD
    col = row - seg * WPAD
    inside = col < geo.wide
    r.mask[0] = jnp.where(inside & (seg < count), 1.0, 0.0)
    r.mask[1] = jnp.where(inside & (seg + 1 < count), 1.0, 0.0)
    r.mask[2] = jnp.where(inside, 1.0, 0.0)
    r.mask[3] = jnp.where(col >= 2, 1.0, 0.0)
    r.mask[4] = jnp.where(col < geo.wide - 2, 1.0, 0.0)


MASKS = 5


def pixel_count(r, geo):
    return r.meta[COUNT].astype(f32) * float(geo.high * geo.wide)


def column_sum(v):
    return jnp.sum(v, axis=0, keepdims=True)


def statistics(pre, cs, r, geo):
    n = pixel_count(r, geo)
    m = r.mask[0]
    total = jnp.zeros((geo.step, LANE), f32)
    for h in range(geo.high):
        total = total + pre[geo.block(h), cs] * m
    mean = column_sum(total) / n
    total = jnp.zeros((geo.step, LANE), f32)
    for h in range(geo.high):
        centred = pre[geo.block(h), cs] - mean
        total = total + centred * centred * m
    return mean, lax.rsqrt(column_sum(total) / n + EPS)


class Slots:
    def __init__(self, arrays, devices, parts, chan_n):
        self.arrays, self.devices, self.parts, self.chan_n = arrays, devices, parts, chan_n

    def operands(self):
        ins = {"slot_dev": (self.devices, SM)}
        for no, array in enumerate(self.arrays):
            ins[f"slots{no}"] = (array, HB)
        return ins

    def start(self, kind, r, dst, sem):
        base = 0
        bases = []
        for array in self.arrays:
            bases.append(base)
            base += array.shape[0]
        for no, row0, tap0, taps in self.parts[kind]:
            ref = getattr(r, f"slots{no}")

            def body(s, carry, ref=ref, base=bases[no], row0=row0, tap0=tap0, taps=taps):
                clip = r.slot_dev[0, base + s]
                chan = r.slot_dev[1, base + s]

                def copy(src, to):
                    pltpu.make_async_copy(src, to, sem).start()

                if kind == "in":
                    copy(
                        ref.at[s, pl.ds(row0, 256)],
                        dst.at[pl.ds(pl.multiple_of(clip * 256, 256), 256), lanes(chan * LANE)],
                    )
                elif kind in ("conv", "conv_t"):
                    rows = pl.ds(pl.multiple_of(clip * 64, 64), 64)
                    src = ref.at[s, pl.ds(row0, taps * 192)].reshape(taps, 3, 64, LANE)
                    if kind == "conv":
                        copy(src, dst.at[pl.ds(tap0, taps), :, rows, lanes(chan * LANE)])
                    else:
                        for b in range(3):
                            copy(
                                src.at[:, b],
                                dst.at[pl.ds(tap0, taps), rows, lanes(chan * LANE + b * 512)],
                            )
                elif kind == "out":
                    for half in range(2):
                        copy(
                            ref.at[s, pl.ds(row0 + half * 128, 128)],
                            dst.at[
                                pl.ds(pl.multiple_of(chan * 128, 128), 128),
                                lanes(clip * 256 + half * 128),
                            ],
                        )
                else:
                    for half in range(2):
                        copy(
                            ref.at[s, pl.ds(row0 + half * 64, 64)],
                            dst.at[
                                pl.ds(pl.multiple_of(clip * 256 + chan * 64, 64), 64),
                                lanes(half * 128),
                            ],
                        )
                return carry

            lax.fori_loop(0, self.arrays[no].shape[0], body, 0)


class Whole:
    def __init__(self, arrays):
        self.arrays = arrays

    def operands(self):
        return {f"whole_{kind}": (array, HB) for kind, array in self.arrays.items()}

    def start(self, kind, r, dst, sem):
        if kind == "conv_t":
            for b in range(3):
                pltpu.make_async_copy(
                    r.whole_conv.at[:, b], dst.at[:, :, pl.ds(b * 512, 512)], sem
                ).start()
        else:
            pltpu.make_async_copy(getattr(r, f"whole_{kind}"), dst, sem).start()


def arrived(dst, sem):
    pltpu.make_async_copy(dst, dst, sem).wait()


def first_matmul(r, geo, x, weight, pre):
    def body(n, carry):
        cs = lanes(n * CHUNK, CHUNK)
        pre[:, cs] = dot(x[...], weight[:, cs])
        return carry

    lax.fori_loop(0, pre.shape[1] // CHUNK, body, 0)


def conv_matmul(r, geo, g, weight, pre):
    def body(n, carry):
        cs = lanes(n * CHUNK, CHUNK)
        for a in range(3):
            w = weight[a, :, :, cs].reshape(-1, CHUNK)
            part = dot(g[a * geo.step : a * geo.step + geo.rows, :], w)
            pre[:, cs] = part if a == 0 else pre[:, cs] + part
        return carry

    lax.fori_loop(0, pre.shape[1] // CHUNK, body, 0)


def clear_edges(ref, geo, edge):
    zero = jnp.zeros((edge * geo.step, ref.shape[-1]), ref.dtype)
    lead = ref.shape[:-2]
    if lead:
        for i in range(lead[0]):
            ref[i, : edge * geo.step, :] = zero
            ref[i, (geo.high + edge) * geo.step :, :] = zero
    else:
        ref[: edge * geo.step, :] = zero
        ref[(geo.high + edge) * geo.step :, :] = zero


def store_rotated(rot, value, h, r, geo):
    at = slice((h + 2) * geo.step, (h + 3) * geo.step)
    rot[2, at, :] = value
    rot[1, at, :] = rotate(value, -1)
    rot[3, at, :] = rotate(value, 1)
    rot[0, at, :] = rotate(value, -2) * r.mask[3]
    rot[4, at, :] = rotate(value, 2) * r.mask[4]


def gate_forward(r, geo, prm, pre, keep):
    clear_edges(r.rot, geo, 2)
    clear_edges(r.g, geo, 1)
    own = r.meta[OWN]
    width = pre.shape[1]

    def body(c, carry):
        cs = lanes(c * LANE)
        mean, rr = statistics(pre, cs, r, geo)
        gain, shift = prm[0:1, cs], prm[1:2, cs]
        keep.gr1[0:1, cs] = gain * rr
        inside = r.mask[2]
        for h in range(geo.high):
            at = geo.block(h)
            xhat = (pre[at, cs] - mean) * rr
            y = xhat * gain + shift
            s = sigmoid(y)
            act = y * s
            keep.xh1[at, cs] = xhat.astype(bf16)
            keep.d1[at, cs] = (s + act * (1.0 - s)).astype(bf16)
            act = act * inside
            r.act[at, :] = act
            later = jnp.concatenate([act[WPAD:], jnp.zeros((WPAD, LANE), f32)], axis=0)
            diff = (later - act) * r.mask[1]
            store_rotated(r.rot, diff, h, r, geo)

        @pl.when(c == own)
        def _():
            keep.diff[...] = r.rot[2, 2 * geo.step : (2 + geo.high) * geo.step, :]

        for h in range(geo.high):
            at = geo.block(h)
            logit = jnp.zeros((geo.step, LANE), f32)
            for a in range(3):
                for b in range(3):
                    near = r.rot[b + 1, (h + a + 1) * geo.step : (h + a + 2) * geo.step, :]
                    logit = logit + near * prm[2 + 3 * a + b : 3 + 3 * a + b, cs]
                    far = r.rot[2 * b, (h + 2 * a) * geo.step : (h + 2 * a + 1) * geo.step, :]
                    logit = logit + far * prm[11 + 3 * a + b : 12 + 3 * a + b, cs]
            q = sigmoid(logit)
            act = r.act[at, :]
            plus = 1.0 + q
            gated = act * plus
            keep.plus[at, cs] = plus.astype(bf16)
            keep.slope[at, cs] = (act * q * (1.0 - q)).astype(bf16)
            to = slice((h + 1) * geo.step, (h + 2) * geo.step)
            for b in range(3):
                r.g[to, lanes(b * width + c * LANE)] = rotate(gated, b - 1).astype(bf16)
        return carry

    lax.fori_loop(0, width // LANE, body, 0)


def middle_forward(r, geo, prm, pre, act2, keep, transposed):
    own = r.meta[OWN]

    def body(c, carry):
        cs = lanes(c * LANE)
        mean, rr = statistics(pre, cs, r, geo)
        gain, shift = prm[20:21, cs], prm[21:22, cs]
        keep.gr2[0:1, cs] = gain * rr
        for h in range(geo.high):
            at = geo.block(h)
            xhat = (pre[at, cs] - mean) * rr
            y = xhat * gain + shift
            s = sigmoid(y)
            act = y * s
            keep.xh2[at, cs] = xhat.astype(bf16)
            keep.d2[at, cs] = (s + act * (1.0 - s)).astype(bf16)
            act2[at, cs] = act.astype(bf16)

            @pl.when(c == own)
            def _():
                transposed[:, h * geo.step : (h + 1) * geo.step] = jnp.transpose(act).astype(bf16)

        return carry

    lax.fori_loop(0, pre.shape[1] // LANE, body, 0)


def third_forward(r, geo, thr, act2, weight, x, keep):
    def body(n, carry):
        ws = lanes(n * CHUNK, CHUNK)
        r.br[...] = dot(act2[...], weight[:, ws])
        for half in range(CHUNK // LANE):
            ls = slice(half * LANE, (half + 1) * LANE)
            cs = lanes(n * CHUNK + half * LANE)
            mean, rr = statistics(r.br, ls, r, geo)
            gain, shift = thr[0:1, cs], thr[1:2, cs]
            keep.gr3[0:1, cs] = gain * rr
            for h in range(geo.high):
                at = geo.block(h)
                xhat = (r.br[at, ls] - mean) * rr
                y = x[at, cs].astype(f32) + (xhat * gain + shift)
                s = sigmoid(y)
                out = y * s
                keep.xh3[at, cs] = xhat.astype(bf16)
                keep.d3[at, cs] = (s + out * (1.0 - s)).astype(bf16)
                keep.x_next[at, cs] = out.astype(bf16)
        return carry

    lax.fori_loop(0, x.shape[1] // CHUNK, body, 0)


def by_destination(r, parts, body):
    each = parts[0].shape[0]

    def step(j, carry):
        for p, ref in enumerate(parts):
            body(r.meta[ORDER + p * each + j], ref, j)
        return carry

    lax.fori_loop(0, each, step, 0)


def third_both(r, geo, thr, act2, act2_t, weight, x, pg, parts):
    n_pix = pixel_count(r, geo)
    r.ag2[...] = jnp.zeros_like(r.ag2)

    def body(n, ref, place):
        ws = lanes(n * CHUNK, CHUNK)
        r.br[...] = dot(act2[...], weight[:, ws])
        for half in range(CHUNK // LANE):
            ls = slice(half * LANE, (half + 1) * LANE)
            cs = lanes(n * CHUNK + half * LANE)
            mean, rr = statistics(r.br, ls, r, geo)
            gain, shift = thr[0:1, cs], thr[1:2, cs]
            grad = pg[0:1, cs]
            m = r.mask[0]
            pool = jnp.zeros((geo.step, LANE), f32)
            s1 = jnp.zeros((geo.step, LANE), f32)
            s2 = jnp.zeros((geo.step, LANE), f32)
            for h in range(geo.high):
                at = geo.block(h)
                xhat = (r.br[at, ls] - mean) * rr
                y = x[at, cs].astype(f32) + (xhat * gain + shift)
                s = sigmoid(y)
                out = y * s
                d = s + out * (1.0 - s)
                pool = pool + out * m
                e = d * (grad * m)
                s1 = s1 + e
                s2 = s2 + e * xhat
                r.br[at, ls] = xhat
                r.e[at, ls] = e
                r.d3[at, cs] = d.astype(bf16)
            shift_grad, gain_grad = column_sum(s1), column_sum(s2)
            r.pooled[0:1, cs] = column_sum(pool) / n_pix
            r.third_grad[0:1, cs] = gain_grad
            r.third_grad[1:2, cs] = shift_grad
            third_scale(r, geo, ls, gain * rr, shift_grad / n_pix, gain_grad / n_pix)
        third_products(r, geo, act2_t, weight, ws, ref, place)

    by_destination(r, parts, body)


def third_scale(r, geo, ls, scale, mean1, mean2):
    m = r.mask[0]
    for h in range(geo.high):
        at = geo.block(h)
        v = scale * (r.e[at, ls] - m * (mean1 + r.br[at, ls] * mean2))
        r.bg[at, ls] = v.astype(bf16)


def third_products(r, geo, act2_t, weight, ws, ref, place):
    grad = dot(act2_t[...], r.bg[...]).astype(bf16)
    for half in range(CHUNK // LANE):
        ref[place, half * LANE : (half + 1) * LANE, :] = grad[:, half * LANE : (half + 1) * LANE]
    r.ag2[...] += dot_nt(r.bg[...], weight[:, ws])


def conv_backward(r, geo, weight_t, parts):
    clear_edges(r.sg, geo, 1)
    r.sgt[...] = jnp.zeros_like(r.sgt)
    own = r.meta[OWN]
    n_pix = pixel_count(r, geo)
    width = r.ag2.shape[1]
    m = r.mask[0]

    def body(c, carry):
        cs = lanes(c * LANE)
        s1 = jnp.zeros((geo.step, LANE), f32)
        s2 = jnp.zeros((geo.step, LANE), f32)
        for h in range(geo.high):
            at = geo.block(h)
            e = r.ag2[at, cs] * r.d2[at, cs].astype(f32)
            r.e[at, :] = e
            e = e * m
            s1 = s1 + e
            s2 = s2 + e * r.xh2[at, cs].astype(f32)
        shift_grad, gain_grad = column_sum(s1), column_sum(s2)

        @pl.when(c == own)
        def _():
            r.small[0:1, :] = gain_grad
            r.small[1:2, :] = shift_grad

        scale, mean1, mean2 = r.gr2[0:1, cs], shift_grad / n_pix, gain_grad / n_pix
        for h in range(geo.high):
            at = geo.block(h)
            v = scale * (r.e[at, :] - m * (mean1 + r.xh2[at, cs].astype(f32) * mean2))
            to = slice((h + 1) * geo.step, (h + 2) * geo.step)
            for b in range(3):
                r.sg[to, lanes(b * width + c * LANE)] = rotate(v, 1 - b).astype(bf16)

            @pl.when(c == own)
            def _():
                turned = jnp.transpose(v).astype(bf16)
                for a in range(3):
                    if 0 <= h + a - 1 < geo.high:
                        place = (h + a - 1) * geo.step
                        r.sgt[a * LANE : (a + 1) * LANE, place : place + geo.step] = turned

        return carry

    lax.fori_loop(0, width // LANE, body, 0)

    def weight_grad(k, carry):
        gs = lanes(k * CHUNK, CHUNK)
        part = dot(r.sgt[...], r.g[geo.step : geo.step + geo.rows, gs])
        b = k // (width // CHUNK)
        first = (k - b * (width // CHUNK)) * CHUNK
        for a in range(3):
            for half in range(CHUNK // LANE):
                block = part[a * LANE : (a + 1) * LANE, half * LANE : (half + 1) * LANE]
                rows = pl.ds(pl.multiple_of(first + half * LANE, LANE), LANE)
                r.wg[3 * a + b, rows, :] = jnp.transpose(block)
        return carry

    lax.fori_loop(0, 3 * width // CHUNK, weight_grad, 0)

    def hand_out(n, ref, place):
        rows = pl.ds(pl.multiple_of(n * 64, 64), 64)
        for tap in range(9):
            ref[place, tap * 64 : (tap + 1) * 64, :] = r.wg[tap, rows, :].astype(bf16)

    by_destination(r, parts, hand_out)

    def input_grad(n, carry):
        cs = lanes(n * CHUNK, CHUNK)
        rows = pl.ds(pl.multiple_of(n * CHUNK, CHUNK), CHUNK)
        for a in range(3):
            lhs = r.sg[(2 - a) * geo.step : (2 - a) * geo.step + geo.rows, :]
            part = dot_nt(lhs, weight_t[a, rows, :])
            r.gg[:, cs] = part if a == 0 else r.gg[:, cs] + part
        return carry

    lax.fori_loop(0, width // CHUNK, input_grad, 0)


def gate_backward(r, geo, prm):
    clear_edges(r.rot, geo, 2)
    own = r.meta[OWN]
    n_pix = pixel_count(r, geo)
    width = r.gg.shape[1]

    def body(c, carry):
        cs = lanes(c * LANE)
        m = r.mask[0]
        inside = r.mask[2]
        for h in range(geo.high):
            at = geo.block(h)
            grad = r.gg[at, cs] * inside
            r.e[at, :] = grad * r.plus[at, cs].astype(f32)
            store_rotated(r.rot, grad * r.slope[at, cs].astype(f32), h, r, geo)
        s1 = jnp.zeros((geo.step, LANE), f32)
        s2 = jnp.zeros((geo.step, LANE), f32)
        for h in range(geo.high):
            at = geo.block(h)
            back = jnp.zeros((geo.step, LANE), f32)
            for a in range(3):
                for b in range(3):
                    near = r.rot[3 - b, (h + 3 - a) * geo.step : (h + 4 - a) * geo.step, :]
                    back = back + near * prm[2 + 3 * a + b : 3 + 3 * a + b, cs]
                    far = r.rot[4 - 2 * b, (h + 4 - 2 * a) * geo.step : (h + 5 - 2 * a) * geo.step, :]
                    back = back + far * prm[11 + 3 * a + b : 12 + 3 * a + b, cs]
            back = back * r.mask[1]
            earlier = jnp.concatenate([jnp.zeros((WPAD, LANE), f32), back[:-WPAD]], axis=0)
            e = (r.e[at, :] + (earlier - back)) * r.d1[at, cs].astype(f32)
            r.e[at, :] = e
            e = e * m
            s1 = s1 + e
            s2 = s2 + e * r.xh1[at, cs].astype(f32)
        shift_grad, gain_grad = column_sum(s1), column_sum(s2)
        scale, mean1, mean2 = r.gr1[0:1, cs], shift_grad / n_pix, gain_grad / n_pix
        for h in range(geo.high):
            at = geo.block(h)
            v = scale * (r.e[at, :] - m * (mean1 + r.xh1[at, cs].astype(f32) * mean2))
            r.fg[at, cs] = v.astype(bf16)

            @pl.when(c == own)
            def _():
                r.fgt[:, h * geo.step : (h + 1) * geo.step] = jnp.transpose(v).astype(bf16)

        @pl.when(c == own)
        def _():
            r.small[0:1, :] = gain_grad
            r.small[1:2, :] = shift_grad
            for a in range(3):
                for b in range(3):
                    near = jnp.zeros((geo.step, LANE), f32)
                    far = jnp.zeros((geo.step, LANE), f32)
                    for h in range(geo.high):
                        diff = r.diff[geo.block(h), :]
                        near = near + diff * r.rot[3 - b, (h + 3 - a) * geo.step : (h + 4 - a) * geo.step, :]
                        far = far + diff * r.rot[4 - 2 * b, (h + 4 - 2 * a) * geo.step : (h + 5 - 2 * a) * geo.step, :]
                    r.small[2 + 3 * a + b : 3 + 3 * a + b, :] = column_sum(near)
                    r.small[11 + 3 * a + b : 12 + 3 * a + b, :] = column_sum(far)

        return carry

    lax.fori_loop(0, width // LANE, body, 0)


def first_products(r, geo, x, parts):
    def body(n, ref, place):
        part = dot(r.fgt[...], x[:, lanes(n * CHUNK, CHUNK)])
        for half in range(CHUNK // LANE):
            block = part[:, half * LANE : (half + 1) * LANE]
            ref[place, half * LANE : (half + 1) * LANE, :] = jnp.transpose(block).astype(bf16)

    by_destination(r, parts, body)


def third_backward(r, geo, weight_in, weight_out, act2_t, pg, parts):
    n_pix = pixel_count(r, geo)
    own = r.meta[OWN]
    r.ag2[...] = jnp.zeros_like(r.ag2)
    per_own = r.e3.shape[1] // CHUNK

    def body(n, ref, place):
        ws = lanes(n * CHUNK, CHUNK)
        rows = pl.ds(pl.multiple_of(n * CHUNK, CHUNK), CHUNK)
        r.br[...] = dot_nt(r.fg[...], weight_in[rows, :])
        m = r.mask[0]
        for half in range(CHUNK // LANE):
            ls = slice(half * LANE, (half + 1) * LANE)
            cs = lanes(n * CHUNK + half * LANE)
            grad = pg[0:1, cs]
            s1 = jnp.zeros((geo.step, LANE), f32)
            s2 = jnp.zeros((geo.step, LANE), f32)
            for h in range(geo.high):
                at = geo.block(h)
                out_grad = r.br[at, ls] + r.d3_next[at, cs].astype(f32) * (grad * m)
                e = out_grad * r.d3[at, cs].astype(f32)
                xhat = r.xh3[at, cs].astype(f32)
                r.ee[at, ls] = e
                r.br[at, ls] = xhat
                e = e * m
                s1 = s1 + e
                s2 = s2 + e * xhat
            shift_grad, gain_grad = column_sum(s1), column_sum(s2)
            r.third_grad[0:1, cs] = gain_grad
            r.third_grad[1:2, cs] = shift_grad
            scale, mean1, mean2 = r.gr3[0:1, cs], shift_grad / n_pix, gain_grad / n_pix
            for h in range(geo.high):
                at = geo.block(h)
                v = scale * (r.ee[at, ls] - m * (mean1 + r.br[at, ls] * mean2))
                r.bg[at, ls] = v.astype(bf16)
        owner = n // per_own

        @pl.when(owner == own)
        def _():
            r.e3[:, lanes((n - owner * per_own) * CHUNK, CHUNK)] = r.ee[...]

        third_products(r, geo, act2_t, weight_out, ws, ref, place)

    by_destination(r, parts, body)


class Sizes:
    def __init__(self, geo, inner, wide, order_n):
        self.geo, self.inner, self.wide, self.order_n = geo, inner, wide, order_n

    def mask(self):
        return VM((MASKS, self.geo.step, LANE), f32)

    def rot(self):
        return VM((5, (self.geo.high + 4) * self.geo.step, LANE), f32)

    def narrow(self, dtype=bf16):
        return ((self.geo.rows, self.inner), dtype)

    def broad(self, dtype=bf16):
        return ((self.geo.rows, self.wide), dtype)

    def stacked(self):
        return ((self.geo.rows + 2 * self.geo.step, 3 * self.inner), bf16)

    def parts(self, rows):
        return {"away": ((self.order_n // 2, rows, LANE), bf16), "home": ((self.order_n // 2, rows, LANE), bf16)}


def gate_outs(z):
    return {
        "g": z.stacked(),
        "xh1": z.narrow(),
        "d1": z.narrow(),
        "plus": z.narrow(),
        "slope": z.narrow(),
        "diff": ((z.geo.rows, LANE), f32),
        "gr1": ((1, z.inner), f32),
    }


def gate_scratch(z):
    return {"rot": z.rot(), "act": VM((z.geo.rows, LANE), f32), "mask": z.mask()}


def middle_outs(z):
    return {
        "xh2": z.narrow(),
        "d2": z.narrow(),
        "gr2": ((1, z.inner), f32),
        "act2_t": ((LANE, z.geo.rows), bf16),
    }


def kernel_gate(z, meta, source, x, prm):
    geo = z.geo

    def body(r):
        source.start("in", r, r.w_in, r.sem)
        fill_masks(r, geo)
        arrived(r.w_in, r.sem)
        first_matmul(r, geo, r.x, r.w_in, r.pre)
        gate_forward(r, geo, r.prm, r.pre, r)

    return call(
        "gate_forward",
        body,
        {"meta": (meta, SM), **source.operands(), "x": (x, VM), "prm": (prm, VM)},
        gate_outs(z),
        {
            **gate_scratch(z),
            "w_in": VM((z.wide, z.inner), bf16),
            "pre": VM((geo.rows, z.inner), f32),
            "sem": pltpu.SemaphoreType.DMA,
        },
        flops=16_000_000_000,
        nbytes=16_000_000,
    )


def kernel_block(z, meta, source, g, x, prm, thr):
    geo = z.geo

    def body(r):
        source.start("conv", r, r.w_mid, r.sem)
        source.start("out", r, r.w_out, r.sem2)
        fill_masks(r, geo)
        arrived(r.w_mid, r.sem)
        conv_matmul(r, geo, r.g, r.w_mid, r.pre)
        middle_forward(r, geo, r.prm, r.pre, r.act2, r, r.act2_t)
        arrived(r.w_out, r.sem2)
        third_forward(r, geo, r.thr, r.act2, r.w_out, r.x, r)

    return call(
        "block_forward",
        body,
        {"meta": (meta, SM), **source.operands(), "g": (g, VM), "x": (x, VM), "prm": (prm, VM), "thr": (thr, VM)},
        {
            **middle_outs(z),
            "xh3": z.broad(),
            "d3": z.broad(),
            "x_next": z.broad(),
            "gr3": ((1, z.wide), f32),
        },
        {
            "mask": z.mask(),
            "w_mid": VM((3, 3, z.inner, z.inner), bf16),
            "w_out": VM((z.inner, z.wide), bf16),
            "pre": VM((geo.rows, z.inner), f32),
            "act2": VM((geo.rows, z.inner), bf16),
            "br": VM((geo.rows, CHUNK), f32),
            "sem": pltpu.SemaphoreType.DMA,
            "sem2": pltpu.SemaphoreType.DMA,
        },
        flops=16_000_000_000,
        nbytes=16_000_000,
    )


def kernel_top(z, meta, source, x, prm, thr, grad_low, bias):
    geo = z.geo

    def body(r):
        source.start("in", r, r.w_in, r.sem)
        source.start("conv", r, r.w_mid, r.sem2)
        source.start("out", r, r.w_out, r.sem3)
        source.start("head", r, r.w_head, r.sem4)
        fill_masks(r, geo)
        arrived(r.w_in, r.sem)
        first_matmul(r, geo, r.x, r.w_in, r.pre)
        gate_forward(r, geo, r.prm, r.pre, r)
        arrived(r.w_mid, r.sem2)
        conv_matmul(r, geo, r.g, r.w_mid, r.pre)
        middle_forward(r, geo, r.prm, r.pre, r.act2, r, r.act2_t)
        arrived(r.w_out, r.sem3)
        arrived(r.w_head, r.sem4)
        n_pix = pixel_count(r, geo)
        r.pg[...] = dot_nt(r.grad[...], r.w_head[...])[0:1] / n_pix
        third_both(r, geo, r.thr, r.act2, r.act2_t, r.w_out, r.x, r.pg, [r.away, r.home])
        low = jnp.broadcast_to(r.pooled[...].astype(bf16), (16, z.wide))
        r.logits[...] = dot(low, r.w_head[...])[0:8] + r.bias[...]

    return call(
        "top_both",
        body,
        {
            "meta": (meta, SM),
            **source.operands(),
            "x": (x, VM),
            "prm": (prm, VM),
            "thr": (thr, VM),
            "grad": (grad_low, VM),
            "bias": (bias, VM),
        },
        {
            **gate_outs(z),
            **middle_outs(z),
            "d3": z.broad(),
            "pooled": ((1, z.wide), f32),
            "pg": ((1, z.wide), f32),
            "logits": ((8, bias.shape[1]), f32),
            "third_grad": ((2, z.wide), f32),
            "ag2": z.narrow(f32),
            **z.parts(256),
        },
        {
            **gate_scratch(z),
            "w_in": VM((z.wide, z.inner), bf16),
            "w_mid": VM((3, 3, z.inner, z.inner), bf16),
            "w_out": VM((z.inner, z.wide), bf16),
            "w_head": VM((z.wide, bias.shape[1]), bf16),
            "pre": VM((geo.rows, z.inner), f32),
            "act2": VM((geo.rows, z.inner), bf16),
            "br": VM((geo.rows, CHUNK), f32),
            "e": VM((geo.rows, CHUNK), f32),
            "bg": VM((geo.rows, CHUNK), bf16),
            "sem": pltpu.SemaphoreType.DMA,
            "sem2": pltpu.SemaphoreType.DMA,
            "sem3": pltpu.SemaphoreType.DMA,
            "sem4": pltpu.SemaphoreType.DMA,
        },
        flops=40_000_000_000,
        nbytes=30_000_000,
    )


def kernel_conv_back(z, meta, source, ag2, kept):
    geo = z.geo

    def body(r):
        source.start("conv_t", r, r.w_t, r.sem)
        fill_masks(r, geo)
        arrived(r.w_t, r.sem)
        conv_backward(r, geo, r.w_t, [r.away, r.home])

    return call(
        "conv_backward",
        body,
        {
            "meta": (meta, SM),
            **source.operands(),
            "ag2": (ag2, VM),
            "xh2": (kept["xh2"], VM),
            "d2": (kept["d2"], VM),
            "gr2": (kept["gr2"], VM),
            "g": (kept["g"], VM),
        },
        {"gg": z.narrow(f32), "small": ((2, LANE), f32), **z.parts(576)},
        {
            "mask": z.mask(),
            "w_t": VM((3, z.inner, 3 * z.inner), bf16),
            "sg": VM(*z.stacked()),
            "sgt": VM((3 * LANE, geo.rows), bf16),
            "wg": VM((9, z.inner, LANE), f32),
            "e": VM((geo.rows, LANE), f32),
            "sem": pltpu.SemaphoreType.DMA,
        },
        flops=20_000_000_000,
        nbytes=16_000_000,
    )


def gate_back_ins(kept, prm):
    ins = {name: (kept[name], VM) for name in ("xh1", "d1", "plus", "slope", "diff", "gr1")}
    ins["prm"] = (prm, VM)
    return ins


def gate_back_scratch(z):
    return {
        "mask": z.mask(),
        "rot": z.rot(),
        "e": VM((z.geo.rows, LANE), f32),
        "fg": VM(*z.narrow()),
        "fgt": VM((LANE, z.geo.rows), bf16),
        "w_in": VM((z.wide, z.inner), bf16),
        "sem": pltpu.SemaphoreType.DMA,
    }


def kernel_join(z, meta, source, source_below, gg, kept, below, prm, x, d3_next, pg):
    geo = z.geo
    both = {}
    for tag, item in (("a_", source), ("b_", source_below)):
        both.update({tag + name: value for name, value in item.operands().items()})

    def view(r, tag):
        picked = {k[2:]: v for k, v in vars(r).items() if k.startswith(tag)}
        return types.SimpleNamespace(**picked)

    def body(r):
        source.start("in", view(r, "a_"), r.w_in, r.sem)
        source_below.start("out", view(r, "b_"), r.w_out, r.sem2)
        fill_masks(r, geo)
        gate_backward(r, geo, r.prm)
        first_products(r, geo, r.x, [r.away_in, r.home_in])
        arrived(r.w_in, r.sem)
        arrived(r.w_out, r.sem2)
        third_backward(r, geo, r.w_in, r.w_out, r.act2_t, r.pg, [r.away, r.home])

    parts = z.parts(256)
    return call(
        "join_backward",
        body,
        {
            "meta": (meta, SM),
            **both,
            "gg": (gg, VM),
            **gate_back_ins(kept, prm),
            "x": (x, VM),
            "d3_next": (d3_next, VM),
            "pg": (pg, VM),
            "d3": (below["d3"], VM),
            "xh3": (below["xh3"], VM),
            "gr3": (below["gr3"], VM),
            "act2_t": (below["act2_t"], VM),
        },
        {
            "small": ((20, LANE), f32),
            "third_grad": ((2, z.wide), f32),
            "ag2": z.narrow(f32),
            "e3": ((geo.rows, z.wide // 4), f32),
            **parts,
            **{name + "_in": value for name, value in parts.items()},
        },
        {
            **gate_back_scratch(z),
            "w_out": VM((z.inner, z.wide), bf16),
            "br": VM((geo.rows, CHUNK), f32),
            "ee": VM((geo.rows, CHUNK), f32),
            "bg": VM((geo.rows, CHUNK), bf16),
            "sem2": pltpu.SemaphoreType.DMA,
        },
        flops=20_000_000_000,
        nbytes=30_000_000,
    )


def kernel_bottom(z, meta, source, gg, kept, prm, x, e3):
    geo = z.geo
    quarter = e3.shape[1]

    def body(r):
        source.start("in", r, r.w_in, r.sem)
        fill_masks(r, geo)
        gate_backward(r, geo, r.prm)
        first_products(r, geo, r.x, [r.away, r.home])
        arrived(r.w_in, r.sem)
        own = r.meta[OWN]
        for n in range(quarter // CHUNK):
            cs = slice(n * CHUNK, (n + 1) * CHUNK)
            rows = pl.ds(pl.multiple_of(own * quarter + n * CHUNK, CHUNK), CHUNK)
            r.x_grad[:, cs] = (dot_nt(r.fg[...], r.w_in[rows, :]) + r.e3[:, cs]).astype(bf16)

    return call(
        "bottom_backward",
        body,
        {
            "meta": (meta, SM),
            **source.operands(),
            "gg": (gg, VM),
            **gate_back_ins(kept, prm),
            "x": (x, VM),
            "e3": (e3, VM),
        },
        {"small": ((20, LANE), f32), "x_grad": ((geo.rows, quarter), bf16), **z.parts(256)},
        gate_back_scratch(z),
        flops=10_000_000_000,
        nbytes=16_000_000,
    )


def local(
    clip_input,
    seg_count,
    proj_in_master,
    conv_master,
    proj_out_master,
    head_master,
    gain_first,
    shift_first,
    taps_near,
    taps_far,
    gain_second,
    shift_second,
    gain_third,
    shift_third,
    head_bias,
    logit_grad,
    clip_n,
    chan_n,
):
    clip = lax.axis_index("clip")
    chan = lax.axis_index("chan")
    _, seg, high, wide_map, wide = clip_input.shape
    layers = proj_in_master.shape[0]
    inner = proj_in_master.shape[2] * chan_n
    classes = head_master.shape[1]
    class_pad = -(-classes // LANE) * LANE
    geo = Geometry(seg, high, wide_map)
    order_n = wide // CHUNK
    z = Sizes(geo, inner, wide, order_n)

    own_small = jnp.concatenate(
        [
            gain_first[:, None],
            shift_first[:, None],
            taps_near.reshape(layers, 9, -1),
            taps_far.reshape(layers, 9, -1),
            gain_second[:, None],
            shift_second[:, None],
            gain_third.reshape(layers, -1, LANE),
            shift_third.reshape(layers, -1, LANE),
        ],
        axis=1,
    )
    all_small = lax.all_gather(own_small, "chan", axis=0, tiled=False)
    prm = jnp.transpose(all_small[:, :, :22], (1, 2, 0, 3)).reshape(layers, 22, inner)
    thr = jnp.transpose(all_small[:, :, 22:].reshape(chan_n, layers, 2, -1), (1, 2, 0, 3)).reshape(
        layers, 2, wide
    )

    head_low = jnp.pad(head_master.astype(bf16), ((0, 0), (0, class_pad - classes)))
    sources = []
    if proj_in_master.shape[1] == 256 and chan_n == 4:
        own_head = lax.dynamic_slice_in_dim(head_low, chan * 64, 64, 0)
        own_head = jnp.transpose(own_head.reshape(64, 2, LANE), (1, 0, 2)).reshape(128, LANE)
        numbers = jnp.arange(clip_n * chan_n, dtype=jnp.int32)
        devices = jnp.stack([numbers // chan_n, numbers % chan_n])
        for layer in range(layers):
            out_low = proj_out_master[layer].astype(bf16)
            items = [
                proj_in_master[layer].astype(bf16),
                conv_master[layer].astype(bf16).reshape(-1, LANE),
                jnp.transpose(out_low.reshape(LANE, 2, LANE), (1, 0, 2)).reshape(256, LANE),
            ]
            if layer == layers - 1:
                items.append(own_head)
            packed = lax.all_gather(jnp.concatenate(items, axis=0), ("clip", "chan"), axis=0, tiled=False)
            parts = {"in": [(0, 0, 0, 0)], "conv": [(0, 256, 0, 3)], "out": [(0, 832, 0, 0)], "head": [(0, 1088, 0, 0)]}
            parts["conv_t"] = parts["conv"]
            sources.append(Slots([packed], devices, parts, chan_n))
    else:
        whole_head = lax.all_gather(head_low, "clip", axis=0, tiled=True)
        gathered = []
        for master, clip_axis, chan_axis in ((proj_in_master, 1, 2), (conv_master, 3, 4), (proj_out_master, 2, 1)):
            item = lax.all_gather(master.astype(bf16), "clip", axis=clip_axis, tiled=True)
            gathered.append(lax.all_gather(item, "chan", axis=chan_axis, tiled=True))
        for layer in range(layers):
            sources.append(
                Whole(
                    {
                        "in": gathered[0][layer],
                        "conv": gathered[1][layer],
                        "out": gathered[2][layer],
                        "head": whole_head,
                    }
                )
            )

    order = jnp.arange(order_n, dtype=jnp.int32)
    meta = jnp.concatenate([seg_count.astype(jnp.int32), chan[None].astype(jnp.int32), order])

    grad_low = logit_grad.astype(bf16)
    grad_rows = jnp.pad(grad_low, ((0, 15), (0, class_pad - classes)))
    bias_row = jnp.pad(head_bias, (0, class_pad - classes))[None]

    x0 = jnp.transpose(clip_input[0], (1, 0, 2, 3))
    x0 = jnp.pad(x0, ((0, 0), (0, 0), (0, WPAD - wide_map), (0, 0))).reshape(geo.rows, wide)

    gate0 = kernel_gate(z, meta, sources[0], x0, prm[0])
    block0 = kernel_block(z, meta, sources[0], gate0["g"], x0, prm[0], thr[0])
    x1 = block0["x_next"]
    top = kernel_top(z, meta, sources[1], x1, prm[1], thr[1], grad_rows, bias_row)
    mid1 = kernel_conv_back(z, meta, sources[1], top["ag2"], top)
    join = kernel_join(
        z, meta, sources[1], sources[0], mid1["gg"], top, block0, prm[1], x1, top["d3"], top["pg"]
    )
    mid0 = kernel_conv_back(z, meta, sources[0], join["ag2"], {**gate0, **block0})
    low = kernel_bottom(z, meta, sources[0], mid0["gg"], gate0, prm[0], x0, join["e3"])

    logits = top["logits"][0:1, :classes]
    input_grad = low["x_grad"].reshape(high, seg, WPAD, -1)[:, :, :wide_map]
    input_grad = jnp.transpose(input_grad, (1, 0, 2, 3))[None]

    pooled_all = lax.all_gather(top["pooled"].astype(bf16), "clip", axis=0, tiled=True)
    grad_all = lax.all_gather(grad_low, "clip", axis=0, tiled=True)
    own_rows = head_master.shape[0]
    pooled_own = lax.dynamic_slice_in_dim(pooled_all, clip * own_rows, own_rows, 1)
    head_share = lax.dot_general(
        pooled_own, grad_all, (((0,), (0,)), ((), ())), preferred_element_type=f32
    )
    bias_grad = jnp.sum(grad_all.astype(f32), axis=0)

    def joined(item, tag=""):
        return jnp.concatenate([item["away" + tag], item["home" + tag]], axis=0)

    in_terms = jnp.stack([joined(low), joined(join, "_in")]).reshape(layers, wide, LANE)
    mid_terms = jnp.stack([joined(mid0), joined(mid1)]).reshape(layers, 8, 3, 3, 64, LANE)
    mid_terms = jnp.transpose(mid_terms, (0, 2, 3, 1, 4, 5)).reshape(layers, 3, 3, inner, LANE)
    out_terms = jnp.stack([joined(join), joined(top)]).reshape(layers, 8, 2, LANE, LANE)
    out_terms = jnp.transpose(out_terms, (0, 3, 1, 2, 4)).reshape(layers, LANE, wide)
    in_share = lax.psum_scatter(in_terms, "clip", scatter_dimension=1, tiled=True).astype(f32)
    mid_share = lax.psum_scatter(mid_terms, "clip", scatter_dimension=3, tiled=True).astype(f32)
    out_share = lax.psum_scatter(out_terms, "clip", scatter_dimension=2, tiled=True).astype(f32)

    third = jnp.stack([join["third_grad"], top["third_grad"]])
    third_own = lax.dynamic_slice_in_dim(third, chan * (wide // chan_n), wide // chan_n, 2)
    small = jnp.concatenate(
        [
            jnp.stack([low["small"], join["small"]]),
            jnp.stack([mid0["small"], mid1["small"]]),
            third_own.reshape(layers, -1, LANE),
        ],
        axis=1,
    )
    small = lax.psum(small, "clip")
    third_rows = (small.shape[1] - 22) // 2
    return (
        logits,
        input_grad,
        in_share,
        mid_share,
        out_share,
        head_share,
        small[:, 0],
        small[:, 1],
        small[:, 2:11].reshape(layers, 3, 3, LANE),
        small[:, 11:20].reshape(layers, 3, 3, LANE),
        small[:, 20],
        small[:, 21],
        small[:, 22 : 22 + third_rows].reshape(layers, -1),
        small[:, 22 + third_rows :].reshape(layers, -1),
        bias_grad,
    )


def solution(mesh):
    clip_n, chan_n = mesh.shape["clip"], mesh.shape["chan"]

    def program(*args):
        return local(*args, clip_n, chan_n)

    in_specs = (
        P("clip", None, None, None, None),
        P("clip"),
        P(None, "clip", "chan"),
        P(None, None, None, "clip", "chan"),
        P(None, "chan", "clip"),
        P("clip", None),
        P(None, "chan"),
        P(None, "chan"),
        P(None, None, None, "chan"),
        P(None, None, None, "chan"),
        P(None, "chan"),
        P(None, "chan"),
        P(None, "chan"),
        P(None, "chan"),
        P(),
        P("clip", None),
    )
    out_specs = (
        P("clip", None),
        P("clip", None, None, None, "chan"),
        P(None, "clip", "chan"),
        P(None, None, None, "clip", "chan"),
        P(None, "chan", "clip"),
        P("clip", None),
        P(None, "chan"),
        P(None, "chan"),
        P(None, None, None, "chan"),
        P(None, None, None, "chan"),
        P(None, "chan"),
        P(None, "chan"),
        P(None, "chan"),
        P(None, "chan"),
        P(),
    )
    return jax.shard_map(program, mesh=mesh, in_specs=in_specs, out_specs=out_specs, check_vma=False)
```

time: 875 us -> 518 us (0.59)
  waiting for transfers between devices: 597 us -> 205 us
  Pallas kernels: 0 us -> 161 us
  matrix products: 52.2 us -> 0.9 us
  local copies, waits for them, and re-layouts: 58.9 us -> 27.7 us
  other arithmetic: 49.5 us -> 18.6 us
    reduce_scatter x8 -> x3, waiting for transfers between devices: 353 us -> 104 us  [the longest x1 70 us: local(): lax.psum_scatter(mid_terms, 'clip', scatter_dimension=3, tiled=True)]
    pallas_call x0 -> x7, Pallas kernels: none -> 161 us  [call(): pl.pallas_call(kernel, name=name, out_shape=[jax.ShapeDtypeStruct(*outs[n...]
    all_gather x6 -> x2, waiting for transfers between devices: 200 us -> 101 us  [local(): lax.all_gather(jnp.concatenate(items, axis=0), ('clip', 'chan'), axis=0,...]
    unnamed x321 -> x72, local copies, waits for them, and re-layouts: 58.7 us -> 8.12 us
    unnamed x18 -> x5, waiting for transfers between devices: 44.4 us -> 0.08 us
    dot_general x32 -> x1, matrix products: 44.4 us -> 0.9 us  [local(): lax.dot_general(pooled_own, grad_all, (((0,), (0,)), ((), ())), preferred...]
    reduce_sum x21 -> x1, other arithmetic: 19.1 us -> 0.58 us  [local(): bias_grad = jnp.sum(grad_all.astype(f32), axis=0)]
    convert_element_type x16 -> x4, other arithmetic: 15.3 us -> 6.02 us  [the longest x1 1.83 us: local(): lax.psum_scatter(mid_terms, 'clip', scatter_dimension=3, tiled=True)]
  transfers between devices with their start and end apart: 16 -> 5, of which waited for: 15 -> 4; matrix products, arithmetic and copies ran while one was open for 6% -> 6% of each run, Pallas kernels for 0% -> 8%
where the time goes in v1:
time: 518 us; the launch traced here: 515 us
  waiting for transfers between devices  205 us (40%)
  Pallas kernels  161 us (31%)
  blocking collectives  86.3 us (17%)
  local copies, waits for them, and re-layouts  27.7 us (5%)
  other arithmetic  18.6 us (4%)
  between operations  15 us (3%)
    pallas_call x7, Pallas kernels, call(): pl.pallas_call(kernel, name=name, out_shape=[jax.ShapeDtypeStruct(*outs[n...  161 us
    all_gather x2, waiting for transfers between devices, local(): lax.all_gather(jnp.concatenate(items, axis=0), ('clip', 'chan'), axis=0,...  101 us
    reduce_scatter x1, waiting for transfers between devices, local(): lax.psum_scatter(mid_terms, 'clip', scatter_dimension=3, tiled=True)  70 us
    reduce_scatter x1, waiting for transfers between devices, local(): lax.psum_scatter(out_terms, 'clip', scatter_dimension=2, tiled=True)  33.7 us
    psum x1, blocking collectives, local(): small = lax.psum(small, 'clip')  33.1 us
    all_gather x1, blocking collectives, local(): lax.all_gather(top['pooled'].astype(bf16), 'clip', axis=0, tiled=True)  30.6 us
    all_gather x1, blocking collectives, local(): grad_all = lax.all_gather(grad_low, 'clip', axis=0, tiled=True)  16.4 us
  transfers between devices with their start and end apart: 5, of which 4 were waited for; matrix products, arithmetic and copies ran while one was open for 6% of the time, Pallas kernels for 8%

profile of v1, /device:TPU:8, one launch (start us, length us, event | category | flops | bytes accessed | tf_op | source)
XLA Modules:
  0.0 515.3 jit_solution(4413118221716914468)
XLA Ops:
  7.2 1.0 convert.14
  8.2 0.7 fusion.5
  8.9 1.3 convert.13
  10.2 1.0 convert.12
  11.1 0.6 slice_bitcast_fusion.1
  11.8 1.5 convert_element_type.63
  13.3 0.8 copy.83
  14.1 1.6 pad_maximum_fusion.8
  15.8 0.9 convert_element_type.60
  16.9 0.9 convert_element_type.59
  17.8 1.6 pad_maximum_fusion.7
  20.2 3.7 copy.98
  24.1 6.1 %all-gather.2 = f32[8,30,128]{2,1,0:T(8,128)S(1)} all-gather(f32[2,30,128]{2,1,0:T(8,128)S(1)} %copy.85), channel_id=4, replica_groups=mesh['clip'=8,'chan'=4] {'chan'}, dimensions={0}, use_global_device_ids=true | all-gather | bytes 153600 | tf_op jit(solution)/shard_map/all_gather | solution.py:982
  30.6 0.6 copy.99
  31.3 0.6 copy.100
  31.9 5.0 pad.17.clone
  37.5 0.6 pad.18.refs_6_
  39.8 0.6 fusion.8
  40.4 56.5 %all-gather.10.cloned.1.call-done = bf16[34816,128]{1,0:T(8,128)(2,1)} async-done(((bf16[1088,128]{1,0:T(8,128)(2,1)}), bf16[34816,128]{1,0:T(8,128)(2,1)}) %all-gather.10.cloned.1.call-update) | async-done | bytes 8912912 | tf_op jit(solution)/shard_map/all_gather | solution.py:1004
  97.0 14.3 %gate_forward.1 = (bf16[1152,1536]{1,0:T(8,128)(2,1)}, bf16[896,512]{1,0:T(8,128)(2,1)}, bf16[896,512]{1,0:T(8,128)(2,1)}, bf16[896,512]{1,0:T(8,128)(2,1)}, bf1...) custom-call(s32[10]{0:T(128)} %pad_add_fusion.1.refs_0_, s32[2,32]{1,0:T(2,128)} %pad_add_fusion.refs_1_.refs_3_, ...), custom_call_target="tpu_custom_call" | custom-call | flops 16000000000 | bytes 16000000 | tf_op jit(solution)/shard_map/gate_forward/pallas_call | solution.py:24
  111.3 27.1 %block_forward.1 = (bf16[896,512]{1,0:T(8,128)(2,1)}, bf16[896,512]{1,0:T(8,128)(2,1)}, f32[1,512]{1,0:T(1,128)}, bf16[128,896]{1,0:T(8,128)(2,1)}, bf16[896,204...) custom-call(s32[10]{0:T(128)} %pad_add_fusion.1.refs_0_, ...), custom_call_target="tpu_custom_call" | custom-call | flops 16000000000 | bytes 16000000 | tf_op jit(solution)/shard_map/block_forward/pallas_call | solution.py:24
  138.4 44.9 %all-gather.8.cloned.1.call-done = bf16[38912,128]{1,0:T(8,128)(2,1)} async-done(((bf16[1216,128]{1,0:T(8,128)(2,1)}), bf16[38912,128]{1,0:T(8,128)(2,1)}) %all-gather.8.cloned.1.call-update) | async-done | bytes 9961488 | tf_op jit(solution)/shard_map/all_gather | solution.py:1004
  183.3 43.3 %top_both.1 = (bf16[1152,1536]{1,0:T(8,128)(2,1)}, bf16[896,512]{1,0:T(8,128)(2,1)}, bf16[896,512]{1,0:T(8,128)(2,1)}, bf16[896,512]{1,0:T(8,128)(2,1)}, bf16[89...) custom-call(s32[10]{0:T(128)} %pad_add_fusion.1.refs_0_, ...), custom_call_target="tpu_custom_call" | custom-call | flops 40000000000 | bytes 30000000 | tf_op jit(solution)/shard_map/top_both/pallas_call | solution.py:24
  226.6 16.6 %conv_backward.2 = (f32[896,512]{1,0:T(8,128)}, f32[2,128]{1,0:T(2,128)}, bf16[4,576,128]{2,1,0:T(8,128)(2,1)}, bf16[4,576,128]{2,1,0:T(8,128)(2,1)}) custom-call(s32[10]{0:T(128)} %pad_add_fusion.1.refs_0_, s32[2,32]{1,0:T(2,128)} %pad_add_fusion.refs_1_.refs_3_, bf16[32,1216,128]{2,1,0:T(8,128)(2,1)} %bitcast.152, f32[896,512]{1,0:T(8,128)} %get-tuple-element.71.refs_3_, ...), custom_call_target="tpu_custom_call" | custom-call | flops 20000000000 | bytes 16000000 | tf_op jit(solution)/shard_map/conv_backward/pallas_call | solution.py:24
  243.2 29.7 %join_backward.1 = (f32[20,128]{1,0:T(8,128)}, f32[2,2048]{1,0:T(2,128)}, f32[896,512]{1,0:T(8,128)}, f32[896,512]{1,0:T(8,128)}, bf16[4,256,128]{2,1,0:T(8,128)...) custom-call(s32[10]{0:T(128)} %pad_add_fusion.1.refs_0_, ...), custom_call_target="tpu_custom_call" | custom-call | flops 20000000000 | bytes 30000000 | tf_op jit(solution)/shard_map/join_backward/pallas_call | solution.py:24
  272.9 1.1 pad_maximum_fusion.4
  274.0 16.6 %conv_backward.3 = (f32[896,512]{1,0:T(8,128)}, f32[2,128]{1,0:T(2,128)}, bf16[4,576,128]{2,1,0:T(8,128)(2,1)}, bf16[4,576,128]{2,1,0:T(8,128)(2,1)}) custom-call(s32[10]{0:T(128)} %pad_add_fusion.1.refs_0_, s32[2,32]{1,0:T(2,128)} %pad_add_fusion.refs_1_.refs_3_, bf16[32,1088,128]{2,1,0:T(8,128)(2,1)} %bitcast.157, f32[896,512]{1,0:T(8,128)} %get-tuple-element.89.refs_3_, ...), custom_call_target="tpu_custom_call" | custom-call | flops 20000000000 | bytes 16000000 | tf_op jit(solution)/shard_map/conv_backward/pallas_call | solution.py:24
  290.7 13.7 %bottom_backward.1 = (f32[20,128]{1,0:T(8,128)}, bf16[896,512]{1,0:T(8,128)(2,1)}, bf16[4,256,128]{2,1,0:T(8,128)(2,1)}, bf16[4,256,128]{2,1,0:T(8,128)(2,1)}) custom-call(s32[10]{0:T(128)} %pad_add_fusion.1.refs_0_, s32[2,32]{1,0:T(2,128)} %pad_add_fusion.refs_1_.refs_3_, bf16[32,1088,128]{2,1,0:T(8,128)(2,1)} %bitcast.158, ...), custom_call_target="tpu_custom_call" | custom-call | flops 10000000000 | bytes 16000000 | tf_op jit(solution)/shard_map/bottom_backward/pallas_call | solution.py:24
  304.3 1.1 pad_maximum_fusion.3
  305.5 1.1 pad_maximum_fusion.2
  306.9 1.1 copy.90
  308.0 1.6 reshape.185
  310.2 1.9 copy.89
  312.8 16.4 %all-gather.4 = bf16[8,1,174]{2,1,0:T(2,128)(2,1)S(1)} all-gather(bf16[1,1,174]{2,1,0:T(2,128)(2,1)S(1)} %copy-done.17), channel_id=1, replica_groups=mesh['clip'=8,'chan'=4] {'clip'}, dimensions={0}, use_global_device_ids=true | all-gather | bytes 3132 | tf_op jit(solution)/shard_map/all_gather | solution.py:1052
  329.8 1.3 slice.91
  331.1 1.2 copy.113
  332.3 33.1 %psum.7 = f32[2,30,128]{2,1,0:T(8,128)S(1)} all-reduce(f32[2,30,128]{2,1,0:T(8,128)S(1)} %pad_maximum_fusion.9), channel_id=1, replica_groups=mesh['clip'=8,'chan'=4] {'clip'}, use_global_device_ids=true, to_apply=%region_3.4 | all-reduce | flops 7680 | bytes 61440 | tf_op jit(solution)/shard_map/psum | solution.py:1082
  365.5 0.6 copy.92
  366.1 0.6 copy.93
  366.7 0.6 copy.115
  367.3 0.6 copy.114
  367.9 30.6 %all-gather.3 = bf16[8,1,2048]{2,1,0:T(2,128)(2,1)S(1)} all-gather(bf16[1,1,2048]{2,1,0:T(2,128)(2,1)S(1)} %convert_bitcast_fusion), channel_id=1, replica_groups=mesh['clip'=8,'chan'=4] {'clip'}, dimensions={0}, use_global_device_ids=true | all-gather | bytes 36864 | tf_op jit(solution)/shard_map/all_gather | solution.py:1051
  399.1 0.9 fusion.1
  400.0 1.6 convert_element_type.65
  401.6 33.7 %reduce-scatter.8.cloned.1.call-done = bf16[2,128,256]{2,1,0:T(8,128)(2,1)} async-done(((bf16[2,128,2048]{2,1,0:T(8,128)(2,1)}), bf16[2,128,256]{2,1,0:T(8,128)(2,1)}) %reduce-scatter.8.cloned.1.call-update) | async-done | bytes 131088 | tf_op jit(solution)/shard_map/reduce_scatter | solution.py:1070
  435.3 1.6 convert_element_type.67
  437.0 70.0 %reduce-scatter.6.cloned.1.call-done = bf16[2,3,3,64,128]{4,3,2,1,0:T(8,128)(2,1)} async-done(((bf16[2,3,3,512,128]{4,3,2,1,0:T(8,128)(2,1)}), bf16[2,3,3,64,128]{4,3,2,1,0:T(8,128)(2,1)}) %reduce-scatter.6.cloned.1.call-update) | async-done | bytes 294928 | tf_op jit(solution)/shard_map/reduce_scatter | solution.py:1069
  507.0 1.8 convert_element_type.66
  (110 shorter events, 5.9 us)
Async XLA Ops:
  7.2 89.8 %all-gather.10.cloned.1.call-start = ((), (), s32[]{:S(2)}) async-start(), calls=%async_computation.7 | async-start | bytes 9191424 | tf_op jit(solution)/shard_map/all_gather | solution.py:1004
  8.9 11.3 %copy-start = (bf16[1,16,7,7,2048]{4,1,3,2,0:T(8,128)(2,1)S(1)}, bf16[1,16,7,7,2048]{4,1,3,2,0:T(8,128)(2,1)}, u32[]{:S(2)}) copy-start(bf16[1,16,7,7,2048]{4,1,3,2,0:T(8,128)(2,1)} %param.16) | copy-start | bytes 9633796
  15.7 167.5 %all-gather.8.cloned.1.call-start = ((), (), s32[]{:S(2)}) async-start(), calls=%async_computation.6 | async-start | bytes 10272768 | tf_op jit(solution)/shard_map/all_gather | solution.py:1004
  19.4 380.6 %reduce-scatter.4.cloned.1.call-start = ((), (), s32[]{:S(2)}) async-start(), calls=%async_computation.3 | async-start | bytes 1179648 | tf_op jit(solution)/shard_map/reduce_scatter | solution.py:1068
  20.1 3.8 copy-start.23
  20.1 3.8 copy-start.24
  20.1 3.8 copy-start.14
  20.2 3.8 copy-start.15
  20.2 3.8 copy-start.25
  20.2 3.8 copy-start.26
  20.2 3.8 copy-start.18
  20.2 3.8 copy-start.19
  31.9 5.0 copy-start.22
  31.9 6.2 %copy-start.27 = (f32[174]{0:T(256)S(1)}, f32[174]{0:T(256)}, u32[]{:S(2)}) copy-start(f32[174]{0:T(256)} %param.30) | copy-start | bytes 2092
  304.3 2.3 copy-start.6
  304.3 2.3 copy-start.7
  305.5 1.2 copy-start.8
  305.5 1.2 copy-start.9
  306.6 128.7 %reduce-scatter.8.cloned.1.call-start = ((), (), s32[]{:S(2)}) async-start(), calls=%async_computation.5 | async-start | bytes 1179648 | tf_op jit(solution)/shard_map/reduce_scatter | solution.py:1070
  306.9 2.8 copy-start.2
  306.9 2.8 copy-start.3
  308.0 1.8 copy-start.4
  308.0 1.8 copy-start.5
  309.7 197.3 %reduce-scatter.6.cloned.1.call-start = ((), (), s32[]{:S(2)}) async-start(), calls=%async_computation.4 | async-start | bytes 2654208 | tf_op jit(solution)/shard_map/reduce_scatter | solution.py:1069
  312.1 0.7 copy-start.17
  312.1 18.9 %copy-start.1 = (bf16[896,512]{1,0:T(8,128)(2,1)S(1)}, bf16[896,512]{1,0:T(8,128)(2,1)}, u32[]{:S(2)}) copy-start(bf16[896,512]{1,0:T(8,128)(2,1)} %get-tuple-element.101) | copy-start | bytes 2752516
  312.1 20.1 %copy-start.10 = (f32[2,2048]{1,0:T(2,128)S(1)}, f32[2,2048]{1,0:T(2,128)}, u32[]{:S(2)}) copy-start(f32[2,2048]{1,0:T(2,128)} %get-tuple-element.120) | copy-start | bytes 49156
  312.1 20.1 %copy-start.11 = (f32[2,2048]{1,0:T(2,128)S(1)}, f32[2,2048]{1,0:T(2,128)}, u32[]{:S(2)}) copy-start(f32[2,2048]{1,0:T(2,128)} %get-tuple-element.119) | copy-start | bytes 49156
  312.1 20.1 %copy-start.12 = (f32[20,128]{1,0:T(8,128)S(1)}, f32[20,128]{1,0:T(8,128)}, u32[]{:S(2)}) copy-start(f32[20,128]{1,0:T(8,128)} %get-tuple-element.116) | copy-start | bytes 30724
  312.1 20.1 %copy-start.13 = (f32[20,128]{1,0:T(8,128)S(1)}, f32[20,128]{1,0:T(8,128)}, u32[]{:S(2)}) copy-start(f32[20,128]{1,0:T(8,128)} %get-tuple-element.115) | copy-start | bytes 30724
  312.2 20.1 %copy-start.20 = (f32[2,128]{1,0:T(2,128)S(1)}, f32[2,128]{1,0:T(2,128)}, u32[]{:S(2)}) copy-start(f32[2,128]{1,0:T(2,128)} %get-tuple-element.118) | copy-start | bytes 3076
  312.2 20.1 %copy-start.21 = (f32[2,128]{1,0:T(2,128)S(1)}, f32[2,128]{1,0:T(2,128)}, u32[]{:S(2)}) copy-start(f32[2,128]{1,0:T(2,128)} %get-tuple-element.117) | copy-start | bytes 3076
  312.2 55.7 %copy-start.16 = (f32[1,2048]{1,0:T(1,128)S(1)}, f32[1,2048]{1,0:T(1,128)}, u32[]{:S(2)}) copy-start(f32[1,2048]{1,0:T(1,128)} %get-tuple-element.114) | copy-start | bytes 24580
Sparse Core Ops, SparseCore 0:
  15.8 81.1 all-gather.9
  100.4 82.8 all-gather.7
  306.7 61.9 reduce-scatter.3
  372.4 62.9 reduce-scatter.7
  438.7 68.2 reduce-scatter.5

commit v2 on v1

--- a/solution.py
+++ b/solution.py
@@ -87,6 +87,7 @@
 
 
 MASKS = 5
+SMALL_ROWS = 24
 
 
 def pixel_count(r, geo):
@@ -127,10 +128,10 @@
         for array in self.arrays:
             bases.append(base)
             base += array.shape[0]
-        for no, row0, tap0, taps in self.parts[kind]:
+        for no, row0, first, many in self.parts[kind]:
             ref = getattr(r, f"slots{no}")
 
-            def body(s, carry, ref=ref, base=bases[no], row0=row0, tap0=tap0, taps=taps):
+            def body(s, carry, ref=ref, base=bases[no], row0=row0, first=first, many=many):
                 clip = r.slot_dev[0, base + s]
                 chan = r.slot_dev[1, base + s]
 
@@ -138,39 +139,30 @@
                     pltpu.make_async_copy(src, to, sem).start()
 
                 if kind == "in":
-                    copy(
-                        ref.at[s, pl.ds(row0, 256)],
-                        dst.at[pl.ds(pl.multiple_of(clip * 256, 256), 256), lanes(chan * LANE)],
-                    )
+                    rows = pl.ds(pl.multiple_of(clip * 256 + first, LANE), many)
+                    copy(ref.at[s, pl.ds(row0, many)], dst.at[rows, lanes(chan * LANE)])
                 elif kind in ("conv", "conv_t"):
                     rows = pl.ds(pl.multiple_of(clip * 64, 64), 64)
-                    src = ref.at[s, pl.ds(row0, taps * 192)].reshape(taps, 3, 64, LANE)
+                    src = ref.at[s, pl.ds(row0, many * 192)].reshape(many, 3, 64, LANE)
                     if kind == "conv":
-                        copy(src, dst.at[pl.ds(tap0, taps), :, rows, lanes(chan * LANE)])
+                        copy(src, dst.at[pl.ds(first, many), :, rows, lanes(chan * LANE)])
                     else:
                         for b in range(3):
                             copy(
                                 src.at[:, b],
-                                dst.at[pl.ds(tap0, taps), rows, lanes(chan * LANE + b * 512)],
+                                dst.at[pl.ds(first, many), rows, lanes(chan * LANE + b * 512)],
                             )
                 elif kind == "out":
+                    rows = pl.ds(pl.multiple_of(chan * LANE, LANE), LANE)
                     for half in range(2):
                         copy(
-                            ref.at[s, pl.ds(row0 + half * 128, 128)],
-                            dst.at[
-                                pl.ds(pl.multiple_of(chan * 128, 128), 128),
-                                lanes(clip * 256 + half * 128),
-                            ],
+                            ref.at[s, pl.ds(row0 + half * LANE, LANE)],
+                            dst.at[rows, lanes(clip * 256 + half * LANE)],
                         )
                 else:
+                    rows = pl.ds(pl.multiple_of(clip * 256 + chan * 64, 64), 64)
                     for half in range(2):
-                        copy(
-                            ref.at[s, pl.ds(row0 + half * 64, 64)],
-                            dst.at[
-                                pl.ds(pl.multiple_of(clip * 256 + chan * 64, 64), 64),
-                                lanes(half * 128),
-                            ],
-                        )
+                        copy(ref.at[s, pl.ds(row0 + half * 64, 64)], dst.at[rows, lanes(half * LANE)])
                 return carry
 
             lax.fori_loop(0, self.arrays[no].shape[0], body, 0)
@@ -403,14 +395,18 @@
         r.bg[at, ls] = v.astype(bf16)
 
 
-def third_products(r, geo, act2_t, weight, ws, ref, place):
+def third_products(r, geo, act2_t, weight, ws, ref, place, row0=0):
     grad = dot(act2_t[...], r.bg[...]).astype(bf16)
     for half in range(CHUNK // LANE):
-        ref[place, half * LANE : (half + 1) * LANE, :] = grad[:, half * LANE : (half + 1) * LANE]
+        rows = slice(row0 + half * LANE, row0 + (half + 1) * LANE)
+        ref[place, rows, :] = grad[:, half * LANE : (half + 1) * LANE]
     r.ag2[...] += dot_nt(r.bg[...], weight[:, ws])
 
 
-def conv_backward(r, geo, weight_t, parts):
+HEAD_ROWS = 16
+
+
+def conv_backward(r, geo, weight_t, sem, parts, top):
     clear_edges(r.sg, geo, 1)
     r.sgt[...] = jnp.zeros_like(r.sgt)
     own = r.meta[OWN]
@@ -474,8 +470,14 @@
         rows = pl.ds(pl.multiple_of(n * 64, 64), 64)
         for tap in range(9):
             ref[place, tap * 64 : (tap + 1) * 64, :] = r.wg[tap, rows, :].astype(bf16)
+        if top:
+            pieces = [r.pooled[0:1, lanes(n * CHUNK, CHUNK)], r.grad[0:1, :].astype(f32)]
+            pieces = [v[:, i * LANE : (i + 1) * LANE] for v in pieces for i in range(2)]
+            pieces.append(jnp.zeros((HEAD_ROWS - 4, LANE), f32))
+            ref[place, 576 : 576 + HEAD_ROWS, :] = jnp.concatenate(pieces, axis=0).astype(bf16)
 
     by_destination(r, parts, hand_out)
+    arrived(weight_t, sem)
 
     def input_grad(n, carry):
         cs = lanes(n * CHUNK, CHUNK)
@@ -535,6 +537,7 @@
 
         @pl.when(c == own)
         def _():
+            r.small[SMALL_ROWS - 4 :, :] = jnp.zeros((4, LANE), f32)
             r.small[0:1, :] = gain_grad
             r.small[1:2, :] = shift_grad
             for a in range(3):
@@ -604,7 +607,7 @@
         def _():
             r.e3[:, lanes((n - owner * per_own) * CHUNK, CHUNK)] = r.ee[...]
 
-        third_products(r, geo, act2_t, weight_out, ws, ref, place)
+        third_products(r, geo, act2_t, weight_out, ws, ref, place, 256)
 
     by_destination(r, parts, body)
 
@@ -789,14 +792,15 @@
     )
 
 
-def kernel_conv_back(z, meta, source, ag2, kept):
+def kernel_conv_back(z, meta, source, ag2, kept, grad_low=None):
     geo = z.geo
+    top = grad_low is not None
+    extra = {"pooled": (kept["pooled"], VM), "grad": (grad_low, VM)} if top else {}
 
     def body(r):
         source.start("conv_t", r, r.w_t, r.sem)
         fill_masks(r, geo)
-        arrived(r.w_t, r.sem)
-        conv_backward(r, geo, r.w_t, [r.away, r.home])
+        conv_backward(r, geo, r.w_t, r.sem, [r.away, r.home], top)
 
     return call(
         "conv_backward",
@@ -809,8 +813,9 @@
             "d2": (kept["d2"], VM),
             "gr2": (kept["gr2"], VM),
             "g": (kept["g"], VM),
+            **extra,
         },
-        {"gg": z.narrow(f32), "small": ((2, LANE), f32), **z.parts(576)},
+        {"gg": z.narrow(f32), "small": ((2, LANE), f32), **z.parts(576 + (HEAD_ROWS if top else 0))},
         {
             "mask": z.mask(),
             "w_t": VM((3, z.inner, 3 * z.inner), bf16),
@@ -858,12 +863,11 @@
         source_below.start("out", view(r, "b_"), r.w_out, r.sem2)
         fill_masks(r, geo)
         gate_backward(r, geo, r.prm)
-        first_products(r, geo, r.x, [r.away_in, r.home_in])
+        first_products(r, geo, r.x, [r.away, r.home])
         arrived(r.w_in, r.sem)
         arrived(r.w_out, r.sem2)
         third_backward(r, geo, r.w_in, r.w_out, r.act2_t, r.pg, [r.away, r.home])
 
-    parts = z.parts(256)
     return call(
         "join_backward",
         body,
@@ -881,12 +885,11 @@
             "act2_t": (below["act2_t"], VM),
         },
         {
-            "small": ((20, LANE), f32),
+            "small": ((SMALL_ROWS, LANE), f32),
             "third_grad": ((2, z.wide), f32),
             "ag2": z.narrow(f32),
             "e3": ((geo.rows, z.wide // 4), f32),
-            **parts,
-            **{name + "_in": value for name, value in parts.items()},
+            **z.parts(512),
         },
         {
             **gate_back_scratch(z),
@@ -901,7 +904,7 @@
     )
 
 
-def kernel_bottom(z, meta, source, gg, kept, prm, x, e3):
+def kernel_bottom(z, meta, source, gg, kept, prm, x, e3, smalls):
     geo = z.geo
     quarter = e3.shape[1]
 
@@ -912,6 +915,10 @@
         first_products(r, geo, r.x, [r.away, r.home])
         arrived(r.w_in, r.sem)
         own = r.meta[OWN]
+        both = jnp.concatenate([r.small[...], r.smalls[...]], axis=0).astype(bf16)
+        for ref in (r.away, r.home):
+            for place in range(ref.shape[0]):
+                ref[place, 256:, :] = both
         for n in range(quarter // CHUNK):
             cs = slice(n * CHUNK, (n + 1) * CHUNK)
             rows = pl.ds(pl.multiple_of(own * quarter + n * CHUNK, CHUNK), CHUNK)
@@ -927,12 +934,76 @@
             **gate_back_ins(kept, prm),
             "x": (x, VM),
             "e3": (e3, VM),
+            "smalls": (smalls, VM),
         },
-        {"small": ((20, LANE), f32), "x_grad": ((geo.rows, quarter), bf16), **z.parts(256)},
-        gate_back_scratch(z),
+        {"x_grad": ((geo.rows, quarter), bf16), **z.parts(256 + SMALL_ROWS + smalls.shape[0])},
+        {**gate_back_scratch(z), "small": VM((SMALL_ROWS, LANE), f32)},
         flops=10_000_000_000,
         nbytes=16_000_000,
     )
+
+
+def fold(recv, home, stack_rows=0):
+    slots, rows, _ = home.shape
+    added = rows - stack_rows
+
+    def body(r):
+        for k in range(slots):
+            out = getattr(r, f"s{k}")
+            out[:added] = (r.recv[k, :added].astype(f32) + r.home[k, :added].astype(f32)).astype(bf16)
+            if stack_rows:
+                out[added:rows] = r.home[k, added:]
+                out[rows:] = r.recv[k, added:]
+
+    outs = {f"s{k}": ((rows + stack_rows, LANE), bf16) for k in range(slots)}
+    done = call("fold", body, {"recv": (recv, VM), "home": (home, VM)}, outs, {}, nbytes=4_000_000)
+    return [done[f"s{k}"] for k in range(slots)]
+
+
+class Grid:
+    def __init__(self, clip_n, chan_n):
+        self.clip_n, self.chan_n = clip_n, chan_n
+        self.z_n = clip_n // 2
+
+    def across_x(self, value):
+        return lax.ppermute(value, "clip", [(i, i ^ 1) for i in range(self.clip_n)])
+
+    def along_z(self, value, k):
+        return lax.ppermute(value, "clip", [(i, (i + 2 * k) % self.clip_n) for i in range(self.clip_n)])
+
+    def across_y(self, value):
+        return lax.ppermute(value, "chan", [(i, i ^ 2) for i in range(self.chan_n)])
+
+    def across_core(self, value):
+        return lax.ppermute(value, "chan", [(i, i ^ 1) for i in range(self.chan_n)])
+
+    def scatter(self, away, home, stack_rows=0):
+        shares = fold(self.across_x(away), home, stack_rows)
+        return [shares[0]] + [self.along_z(shares[k], k) for k in range(1, self.z_n)]
+
+    def gather(self, own, cut):
+        clip, chan = lax.axis_index("clip"), lax.axis_index("chan")
+        column = jnp.stack([own] + [self.along_z(own, k) for k in range(1, self.z_n)])
+        over_x, over_y = self.across_x(column), self.across_y(column)
+        low = self.across_y(over_x[:, :cut])
+        high = self.across_x(over_y[:, cut:])
+        arrays = [column, over_x, over_y, low, high]
+        arrays = arrays + [self.across_core(item) for item in arrays]
+        z, x = clip // 2, clip % 2
+        column_z = (z + self.z_n - jnp.arange(self.z_n, dtype=jnp.int32)) % self.z_n
+        clips, chans = [], []
+        for core in (0, 1):
+            for dx, dy in ((0, 0), (1, 0), (0, 2), (1, 2), (1, 2)):
+                clips.append(column_z * 2 + (x ^ dx))
+                chans.append(jnp.full((self.z_n,), 1, jnp.int32) * (chan ^ dy ^ core))
+        devices = jnp.stack([jnp.concatenate(clips), jnp.concatenate(chans)]).astype(jnp.int32)
+        whole = [0, 1, 2, 5, 6, 7]
+        return arrays, devices, whole, [3, 8], [4, 9]
+
+
+def four(shares):
+    a, b, c, d = [v.astype(f32) for v in shares]
+    return (a + c) + (b + d)
 
 
 def local(
@@ -957,14 +1028,17 @@
 ):
     clip = lax.axis_index("clip")
     chan = lax.axis_index("chan")
-    _, seg, high, wide_map, wide = clip_input.shape
+    _, seg, high_map, wide_map, wide = clip_input.shape
     layers = proj_in_master.shape[0]
     inner = proj_in_master.shape[2] * chan_n
     classes = head_master.shape[1]
     class_pad = -(-classes // LANE) * LANE
-    geo = Geometry(seg, high, wide_map)
+    geo = Geometry(seg, high_map, wide_map)
     order_n = wide // CHUNK
     z = Sizes(geo, inner, wide, order_n)
+
+    direct = clip_n == 8 and chan_n == 4 and proj_in_master.shape[1] == 256
+    grid = Grid(clip_n, chan_n)
 
     own_small = jnp.concatenate(
         [
@@ -979,51 +1053,66 @@
         ],
         axis=1,
     )
-    all_small = lax.all_gather(own_small, "chan", axis=0, tiled=False)
+    if direct:
+        empty = jnp.zeros((chan_n,) + own_small.shape, f32)
+        all_small = lax.dynamic_update_slice_in_dim(empty, own_small[None], chan, 0)
+        all_small = all_small + grid.across_y(all_small)
+        all_small = all_small + grid.across_core(all_small)
+    else:
+        all_small = lax.all_gather(own_small, "chan", axis=0, tiled=False)
     prm = jnp.transpose(all_small[:, :, :22], (1, 2, 0, 3)).reshape(layers, 22, inner)
     thr = jnp.transpose(all_small[:, :, 22:].reshape(chan_n, layers, 2, -1), (1, 2, 0, 3)).reshape(
         layers, 2, wide
     )
 
     head_low = jnp.pad(head_master.astype(bf16), ((0, 0), (0, class_pad - classes)))
-    sources = []
-    if proj_in_master.shape[1] == 256 and chan_n == 4:
+    if direct:
         own_head = lax.dynamic_slice_in_dim(head_low, chan * 64, 64, 0)
         own_head = jnp.transpose(own_head.reshape(64, 2, LANE), (1, 0, 2)).reshape(128, LANE)
+        in_low = [proj_in_master[layer].astype(bf16) for layer in range(layers)]
+        mid_low = [conv_master[layer].astype(bf16).reshape(-1, LANE) for layer in range(layers)]
+        out_low = [proj_out_master[layer].astype(bf16).reshape(LANE, 2, LANE) for layer in range(layers)]
+        out_low = [jnp.transpose(item, (1, 0, 2)).reshape(256, LANE) for item in out_low]
+        arrays, devices, full, low, high = grid.gather(in_low[0], 128)
+        parts = {"in": [(i, 0, 0, 256) for i in full]}
+        parts["in"] += [(i, 0, 0, 128) for i in low] + [(i, 0, 128, 128) for i in high]
+        in_source = Slots(arrays, devices, parts, chan_n)
+        arrays, devices, full, low, high = grid.gather(jnp.concatenate([mid_low[0], out_low[0]]), 384)
+        parts = {
+            "conv": [(i, 0, 0, 3) for i in full] + [(i, 0, 0, 2) for i in low] + [(i, 0, 2, 1) for i in high],
+            "out": [(i, 576, 0, 2) for i in full] + [(i, 192, 0, 2) for i in high],
+        }
+        parts["conv_t"] = parts["conv"]
+        rest_source = Slots(arrays, devices, parts, chan_n)
+        packed = jnp.concatenate([in_low[1], mid_low[1], out_low[1], own_head], axis=0)
+        packed = lax.all_gather(packed, ("clip", "chan"), axis=0, tiled=False)
         numbers = jnp.arange(clip_n * chan_n, dtype=jnp.int32)
         devices = jnp.stack([numbers // chan_n, numbers % chan_n])
-        for layer in range(layers):
-            out_low = proj_out_master[layer].astype(bf16)
-            items = [
-                proj_in_master[layer].astype(bf16),
-                conv_master[layer].astype(bf16).reshape(-1, LANE),
-                jnp.transpose(out_low.reshape(LANE, 2, LANE), (1, 0, 2)).reshape(256, LANE),
-            ]
-            if layer == layers - 1:
-                items.append(own_head)
-            packed = lax.all_gather(jnp.concatenate(items, axis=0), ("clip", "chan"), axis=0, tiled=False)
-            parts = {"in": [(0, 0, 0, 0)], "conv": [(0, 256, 0, 3)], "out": [(0, 832, 0, 0)], "head": [(0, 1088, 0, 0)]}
-            parts["conv_t"] = parts["conv"]
-            sources.append(Slots([packed], devices, parts, chan_n))
+        parts = {
+            "in": [(0, 0, 0, 256)],
+            "conv": [(0, 256, 0, 3)],
+            "conv_t": [(0, 256, 0, 3)],
+            "out": [(0, 832, 0, 2)],
+            "head": [(0, 1088, 0, 2)],
+        }
+        top_source = Slots([packed], devices, parts, chan_n)
     else:
         whole_head = lax.all_gather(head_low, "clip", axis=0, tiled=True)
         gathered = []
         for master, clip_axis, chan_axis in ((proj_in_master, 1, 2), (conv_master, 3, 4), (proj_out_master, 2, 1)):
             item = lax.all_gather(master.astype(bf16), "clip", axis=clip_axis, tiled=True)
             gathered.append(lax.all_gather(item, "chan", axis=chan_axis, tiled=True))
-        for layer in range(layers):
-            sources.append(
-                Whole(
-                    {
-                        "in": gathered[0][layer],
-                        "conv": gathered[1][layer],
-                        "out": gathered[2][layer],
-                        "head": whole_head,
-                    }
-                )
-            )
+        in_source = rest_source = Whole(
+            {"in": gathered[0][0], "conv": gathered[1][0], "out": gathered[2][0], "head": whole_head}
+        )
+        top_source = Whole(
+            {"in": gathered[0][1], "conv": gathered[1][1], "out": gathered[2][1], "head": whole_head}
+        )
 
     order = jnp.arange(order_n, dtype=jnp.int32)
+    if direct:
+        z_to = (clip // 2 + jnp.arange(4, dtype=jnp.int32)) % 4
+        order = jnp.concatenate([z_to * 2 + ((clip % 2) ^ 1), z_to * 2 + clip % 2]).astype(jnp.int32)
     meta = jnp.concatenate([seg_count.astype(jnp.int32), chan[None].astype(jnp.int32), order])
 
     grad_low = logit_grad.astype(bf16)
@@ -1033,54 +1122,75 @@
     x0 = jnp.transpose(clip_input[0], (1, 0, 2, 3))
     x0 = jnp.pad(x0, ((0, 0), (0, 0), (0, WPAD - wide_map), (0, 0))).reshape(geo.rows, wide)
 
-    gate0 = kernel_gate(z, meta, sources[0], x0, prm[0])
-    block0 = kernel_block(z, meta, sources[0], gate0["g"], x0, prm[0], thr[0])
+    gate0 = kernel_gate(z, meta, in_source, x0, prm[0])
+    block0 = kernel_block(z, meta, rest_source, gate0["g"], x0, prm[0], thr[0])
     x1 = block0["x_next"]
-    top = kernel_top(z, meta, sources[1], x1, prm[1], thr[1], grad_rows, bias_row)
-    mid1 = kernel_conv_back(z, meta, sources[1], top["ag2"], top)
+    top = kernel_top(z, meta, top_source, x1, prm[1], thr[1], grad_rows, bias_row)
+    mid1 = kernel_conv_back(z, meta, top_source, top["ag2"], top, grad_rows)
     join = kernel_join(
-        z, meta, sources[1], sources[0], mid1["gg"], top, block0, prm[1], x1, top["d3"], top["pg"]
+        z, meta, top_source, rest_source, mid1["gg"], top, block0, prm[1], x1, top["d3"], top["pg"]
     )
-    mid0 = kernel_conv_back(z, meta, sources[0], join["ag2"], {**gate0, **block0})
-    low = kernel_bottom(z, meta, sources[0], mid0["gg"], gate0, prm[0], x0, join["e3"])
+    mid0 = kernel_conv_back(z, meta, rest_source, join["ag2"], {**gate0, **block0})
+    third = jnp.stack([join["third_grad"], top["third_grad"]])
+    third = lax.dynamic_slice_in_dim(third, chan * (wide // chan_n), wide // chan_n, 2)
+    third_rows = wide // chan_n // LANE
+    smalls = [join["small"], mid0["small"], mid1["small"], third.reshape(-1, LANE)]
+    smalls = jnp.concatenate(smalls, axis=0)
+    smalls = jnp.pad(smalls, ((0, -smalls.shape[0] % 16 + 8), (0, 0)))
+    low = kernel_bottom(z, meta, in_source, mid0["gg"], gate0, prm[0], x0, join["e3"], smalls)
 
     logits = top["logits"][0:1, :classes]
-    input_grad = low["x_grad"].reshape(high, seg, WPAD, -1)[:, :, :wide_map]
+    input_grad = low["x_grad"].reshape(high_map, seg, WPAD, -1)[:, :, :wide_map]
     input_grad = jnp.transpose(input_grad, (1, 0, 2, 3))[None]
 
-    pooled_all = lax.all_gather(top["pooled"].astype(bf16), "clip", axis=0, tiled=True)
-    grad_all = lax.all_gather(grad_low, "clip", axis=0, tiled=True)
-    own_rows = head_master.shape[0]
-    pooled_own = lax.dynamic_slice_in_dim(pooled_all, clip * own_rows, own_rows, 1)
-    head_share = lax.dot_general(
-        pooled_own, grad_all, (((0,), (0,)), ((), ())), preferred_element_type=f32
-    )
-    bias_grad = jnp.sum(grad_all.astype(f32), axis=0)
-
-    def joined(item, tag=""):
-        return jnp.concatenate([item["away" + tag], item["home" + tag]], axis=0)
-
-    in_terms = jnp.stack([joined(low), joined(join, "_in")]).reshape(layers, wide, LANE)
-    mid_terms = jnp.stack([joined(mid0), joined(mid1)]).reshape(layers, 8, 3, 3, 64, LANE)
-    mid_terms = jnp.transpose(mid_terms, (0, 2, 3, 1, 4, 5)).reshape(layers, 3, 3, inner, LANE)
-    out_terms = jnp.stack([joined(join), joined(top)]).reshape(layers, 8, 2, LANE, LANE)
-    out_terms = jnp.transpose(out_terms, (0, 3, 1, 2, 4)).reshape(layers, LANE, wide)
-    in_share = lax.psum_scatter(in_terms, "clip", scatter_dimension=1, tiled=True).astype(f32)
-    mid_share = lax.psum_scatter(mid_terms, "clip", scatter_dimension=3, tiled=True).astype(f32)
-    out_share = lax.psum_scatter(out_terms, "clip", scatter_dimension=2, tiled=True).astype(f32)
-
-    third = jnp.stack([join["third_grad"], top["third_grad"]])
-    third_own = lax.dynamic_slice_in_dim(third, chan * (wide // chan_n), wide // chan_n, 2)
-    small = jnp.concatenate(
-        [
-            jnp.stack([low["small"], join["small"]]),
-            jnp.stack([mid0["small"], mid1["small"]]),
-            third_own.reshape(layers, -1, LANE),
-        ],
-        axis=1,
-    )
-    small = lax.psum(small, "clip")
-    third_rows = (small.shape[1] - 22) // 2
+    if direct:
+        out1 = four(grid.scatter(top["away"], top["home"]))
+        mid1_shares = grid.scatter(mid1["away"], mid1["home"], HEAD_ROWS)
+        joined = four(grid.scatter(join["away"], join["home"]))
+        mid0_sum = four(grid.scatter(mid0["away"], mid0["home"]))
+        last = four(grid.scatter(low["away"], low["home"]))
+        in_share = jnp.stack([last[:256], joined[:256]])
+        mid_share = jnp.stack([mid0_sum, four([v[:576] for v in mid1_shares])])
+        mid_share = mid_share.reshape(conv_master.shape)
+        out_share = jnp.stack([joined[256:], out1]).reshape(layers, 2, LANE, LANE)
+        out_share = jnp.transpose(out_share, (0, 2, 1, 3)).reshape(proj_out_master.shape)
+        small = last[256:]
+        heads = jnp.stack([v[576:].reshape(2, HEAD_ROWS, LANE)[:, :4] for v in mid1_shares])
+        heads = heads.reshape(8, 4, LANE)
+        pooled_all, grad_all = heads[:, :2].reshape(8, 256), heads[:, 2:].reshape(8, 256)[:, :classes]
+        head_share = lax.dot_general(
+            pooled_all, grad_all, (((0,), (0,)), ((), ())), preferred_element_type=f32
+        )
+        g = grad_all.astype(f32)
+        g = g[0::2] + g[1::2]
+        bias_grad = (g[0] + g[2]) + (g[1] + g[3])
+    else:
+        pooled_all = lax.all_gather(top["pooled"].astype(bf16), "clip", axis=0, tiled=True)
+        grad_all = lax.all_gather(grad_low, "clip", axis=0, tiled=True)
+        own_rows = head_master.shape[0]
+        pooled_own = lax.dynamic_slice_in_dim(pooled_all, clip * own_rows, own_rows, 1)
+        head_share = lax.dot_general(
+            pooled_own, grad_all, (((0,), (0,)), ((), ())), preferred_element_type=f32
+        )
+        bias_grad = jnp.sum(grad_all.astype(f32), axis=0)
+
+        def joined(item, first, rows):
+            return jnp.concatenate([item["away"], item["home"]], axis=0)[:, first : first + rows]
+
+        in_terms = jnp.stack([joined(low, 0, 256), joined(join, 0, 256)]).reshape(layers, wide, LANE)
+        mid_terms = jnp.stack([joined(mid0, 0, 576), joined(mid1, 0, 576)])
+        mid_terms = mid_terms.reshape(layers, order_n, 3, 3, 64, LANE)
+        mid_terms = jnp.transpose(mid_terms, (0, 2, 3, 1, 4, 5)).reshape(layers, 3, 3, inner, LANE)
+        out_terms = jnp.stack([joined(join, 256, 256), joined(top, 0, 256)])
+        out_terms = out_terms.reshape(layers, order_n, 2, LANE, LANE)
+        out_terms = jnp.transpose(out_terms, (0, 3, 1, 2, 4)).reshape(layers, LANE, wide)
+        in_share = lax.psum_scatter(in_terms, "clip", scatter_dimension=1, tiled=True).astype(f32)
+        mid_share = lax.psum_scatter(mid_terms, "clip", scatter_dimension=3, tiled=True).astype(f32)
+        out_share = lax.psum_scatter(out_terms, "clip", scatter_dimension=2, tiled=True).astype(f32)
+        small = lax.psum(low["home"][0, 256:].astype(f32), "clip")
+    firsts = small[: 2 * SMALL_ROWS].reshape(2, SMALL_ROWS, LANE)
+    seconds = small[2 * SMALL_ROWS : 2 * SMALL_ROWS + 4].reshape(2, 2, LANE)
+    thirds = small[2 * SMALL_ROWS + 4 : 2 * SMALL_ROWS + 4 + 4 * third_rows].reshape(2, 2, -1)
     return (
         logits,
         input_grad,
@@ -1088,14 +1198,14 @@
         mid_share,
         out_share,
         head_share,
-        small[:, 0],
-        small[:, 1],
-        small[:, 2:11].reshape(layers, 3, 3, LANE),
-        small[:, 11:20].reshape(layers, 3, 3, LANE),
-        small[:, 20],
-        small[:, 21],
-        small[:, 22 : 22 + third_rows].reshape(layers, -1),
-        small[:, 22 + third_rows :].reshape(layers, -1),
+        firsts[:, 0],
+        firsts[:, 1],
+        firsts[:, 2:11].reshape(taps_near.shape),
+        firsts[:, 11:20].reshape(taps_far.shape),
+        seconds[:, 0],
+        seconds[:, 1],
+        thirds[:, 0],
+        thirds[:, 1],
         bias_grad,
     )
 

time: 518 us -> 379 us (0.73)
  waiting for transfers between devices: 205 us -> 75.5 us
  blocking collectives: 86.3 us -> 0 us
  starting transfers between devices: 0.21 us -> 50.8 us
  local copies, waits for them, and re-layouts: 27.7 us -> 38.8 us
  Pallas kernels: 161 us -> 168 us
    reduce_scatter x3 -> x0, waiting for transfers between devices: 104 us -> none  [the longest x1 70 us: local(): lax.psum_scatter(mid_terms, 'clip', scatter_dimension=3, tiled=True)]
    all_gather x2 -> x1, waiting for transfers between devices: 101 us -> 0.02 us  [local(): packed = lax.all_gather(packed, ('clip', 'chan'), axis=0, tiled=False)]
    ppermute x0 -> x46, waiting for transfers between devices: none -> 75.5 us  [the longest x9 28.2 us: across_x(): return lax.ppermute(value, 'clip', [(i, i ^ 1) for i in range(self.clip_n)])]
    all_gather x3 -> x0, blocking collectives: 53.2 us -> none  [the longest x1 30.6 us: local(): lax.all_gather(top['pooled'].astype(bf16), 'clip', axis=0, tiled=True)]
    ppermute x0 -> x46, starting transfers between devices: none -> 50.8 us  [the longest x21 32.2 us: along_z(): lax.ppermute(value, 'clip', [(i, (i + 2 * k) % self.clip_n) for i in rang...]
    psum x1 -> x0, blocking collectives: 33.1 us -> none  [local(): small = lax.psum(small, 'clip')]
    unnamed x72 -> x74, local copies, waits for them, and re-layouts: 8.12 us -> 17.3 us
    pallas_call x7 -> x12, Pallas kernels: 161 us -> 168 us  [call(): pl.pallas_call(kernel, name=name, out_shape=[jax.ShapeDtypeStruct(*outs[n...]
  transfers between devices with their start and end apart: 5 -> 47, of which waited for: 4 -> 16; matrix products, arithmetic and copies ran while one was open for 6% -> 12% of each run, Pallas kernels for 8% -> 14%
where the time goes in v2:
time: 379 us; the launch traced here: 372 us
  Pallas kernels  168 us (44%)
  waiting for transfers between devices  75.5 us (20%)
  starting transfers between devices  50.8 us (13%)
  local copies, waits for them, and re-layouts  38.8 us (10%)
  other arithmetic  22.5 us (6%)
  between operations  15.8 us (4%)
    pallas_call x12, Pallas kernels, call(): pl.pallas_call(kernel, name=name, out_shape=[jax.ShapeDtypeStruct(*outs[n...  168 us
    ppermute x21, starting transfers between devices, along_z(): lax.ppermute(value, 'clip', [(i, (i + 2 * k) % self.clip_n) for i in rang...  32.2 us
    ppermute x9, waiting for transfers between devices, across_x(): return lax.ppermute(value, 'clip', [(i, i ^ 1) for i in range(self.clip_n)])  28.2 us
    ppermute x5, waiting for transfers between devices, across_y(): return lax.ppermute(value, 'chan', [(i, i ^ 2) for i in range(self.chan_n)])  25.2 us
    ppermute x21, waiting for transfers between devices, along_z(): lax.ppermute(value, 'clip', [(i, (i + 2 * k) % self.clip_n) for i in rang...  22.1 us
    unnamed x74, local copies, waits for them, and re-layouts  17.3 us
    ppermute x9, starting transfers between devices, across_x(): return lax.ppermute(value, 'clip', [(i, i ^ 1) for i in range(self.clip_n)])  9.39 us
  transfers between devices with their start and end apart: 47, of which 16 were waited for; matrix products, arithmetic and copies ran while one was open for 12% of the time, Pallas kernels for 14%

profile of v2, /device:TPU:8, one launch (start us, length us, event | category | flops | bytes accessed | tf_op | source)
XLA Modules:
  0.0 372.4 jit_solution(7176672240328634009)
XLA Ops:
  13.2 3.0 collective-permute-start.13
  16.3 1.6 fusion.12
  17.9 2.5 collective-permute-start
  22.4 1.5 concatenate.27
  32.9 3.8 %collective-permute-done.1 = bf16[832,128]{1,0:T(8,128)(2,1)} collective-permute-done((bf16[832,128]{1,0:T(8,128)(2,1)}, bf16[832,128]{1,0:T(8,128)(2,1)}, u32[]{:S(2)}, u32[]{:S(2)}) %collective-permute-start.1) | collective-permute-done | bytes 213024 | tf_op jit(solution)/shard_map/ppermute | solution.py:972
  36.7 4.5 %collective-permute-start.12 = (bf16[256,128]{1,0:T(8,128)(2,1)S(1)}, bf16[256,128]{1,0:T(8,128)(2,1)S(1)}, u32[]{:S(2)}, u32[]{:S(2)}) collective-permute-start(bf16[256,128]{1,0:T(8,128)(2,1)S(1)} %bitcast.153), channel_id=1, source_target_pairs={{0,8},{4,12},{8,16},{12,20},{16,24},{20,28},{24,0},{28,4},{1,9},{5... | collective-permute-start | bytes 196616 | tf_op jit(solution)/shard_map/ppermute | solution.py:972
  41.2 4.6 %collective-permute-done = bf16[832,128]{1,0:T(8,128)(2,1)} collective-permute-done((bf16[832,128]{1,0:T(8,128)(2,1)}, bf16[832,128]{1,0:T(8,128)(2,1)}, u32[]{:S(2)}, u32[]{:S(2)}) %collective-permute-start) | collective-permute-done | bytes 213024 | tf_op jit(solution)/shard_map/ppermute | solution.py:972
  45.9 1.5 collective-permute-start.24
  47.4 2.1 pad_maximum_fusion.refs_2_.refs_4_
  52.8 1.5 collective-permute-start.3
  61.5 1.8 copy.96
  64.0 2.9 pad.21.clone
  68.0 11.3 %collective-permute-done.16.refs_4_ = bf16[4,256,128]{2,1,0:T(8,128)(2,1)} collective-permute-done((bf16[4,256,128]{2,1,0:T(8,128)(2,1)S(1)}, bf16[4,256,128]{2,1,0:T(8,128)(2,1)}, u32[]{:S(2)}, u32[]{:S(2)}) %collective-permute-start.16) | collective-permute-done | bytes 262176 | tf_op jit(solution)/shard_map/ppermute | solution.py:975
  80.2 1.6 collective-permute-start.18
  82.8 4.0 %collective-permute-done.15.refs_3_ = bf16[4,256,128]{2,1,0:T(8,128)(2,1)} collective-permute-done((bf16[4,256,128]{2,1,0:T(8,128)(2,1)S(1)}, bf16[4,256,128]{2,1,0:T(8,128)(2,1)}, u32[]{:S(2)}, u32[]{:S(2)}) %collective-permute-start.15) | collective-permute-done | bytes 262176 | tf_op jit(solution)/shard_map/ppermute | solution.py:969
  88.4 1.9 collective-permute-start.17
  92.4 1.9 collective-permute-start.5
  99.3 12.6 %collective-permute-done.5.refs_5_.refs_7_ = bf16[4,384,128]{2,1,0:T(8,128)(2,1)} collective-permute-done((bf16[4,384,128]{2,1,0:T(8,128)(2,1)S(1)}, bf16[4,384,128]{2,1,0:T(8,128)(2,1)}, u32[]{:S(2)}, u32[]{:S(2)}) %collective-permute-start.5) | collective-permute-done | bytes 393248 | tf_op jit(solution)/shard_map/ppermute | solution.py:975
  112.4 14.2 %gate_forward.1 = (bf16[1152,1536]{1,0:T(8,128)(2,1)}, bf16[896,512]{1,0:T(8,128)(2,1)}, bf16[896,512]{1,0:T(8,128)(2,1)}, bf16[896,512]{1,0:T(8,128)(2,1)}, bf1...) custom-call(s32[10]{0:T(128)} %pad_add_fusion.2.refs_0_, s32[2,40]{1,0:T(2,128)} %pad_add_fusion.1.refs_1_.refs_3_, ...), custom_call_target="tpu_custom_call" | custom-call | flops 16000000000 | bytes 16000000 | tf_op jit(solution)/shard_map/gate_forward/pallas_call | solution.py:24
  128.4 27.0 %block_forward.1 = (bf16[896,512]{1,0:T(8,128)(2,1)}, bf16[896,512]{1,0:T(8,128)(2,1)}, f32[1,512]{1,0:T(1,128)}, bf16[128,896]{1,0:T(8,128)(2,1)}, bf16[896,204...) custom-call(s32[10]{0:T(128)} %pad_add_fusion.2.refs_0_, ...), custom_call_target="tpu_custom_call" | custom-call | flops 16000000000 | bytes 16000000 | tf_op jit(solution)/shard_map/block_forward/pallas_call | solution.py:24
  155.5 43.3 %top_both.1 = (bf16[1152,1536]{1,0:T(8,128)(2,1)}, bf16[896,512]{1,0:T(8,128)(2,1)}, bf16[896,512]{1,0:T(8,128)(2,1)}, bf16[896,512]{1,0:T(8,128)(2,1)}, bf16[89...) custom-call(s32[10]{0:T(128)} %pad_add_fusion.2.refs_0_, ...), custom_call_target="tpu_custom_call" | custom-call | flops 40000000000 | bytes 30000000 | tf_op jit(solution)/shard_map/top_both/pallas_call | solution.py:24
  198.8 14.9 %conv_backward.2 = (f32[896,512]{1,0:T(8,128)}, f32[2,128]{1,0:T(2,128)}, bf16[4,592,128]{2,1,0:T(8,128)(2,1)}, bf16[4,592,128]{2,1,0:T(8,128)(2,1)}) custom-call(s32[10]{0:T(128)} %pad_add_fusion.2.refs_0_, s32[2,32]{1,0:T(2,128)} %pad_add_fusion.refs_1_, bf16[32,1216,128]{2,1,0:T(8,128)(2,1)} %bitcast.195, f32[896,512]{1,0:T(8,128)} %get-tuple-element.88.refs_3_, ...), custom_call_target="tpu_custom_call" | custom-call | flops 20000000000 | bytes 16000000 | tf_op jit(solution)/shard_map/conv_backward/pallas_call | solution.py:24
  213.8 29.9 %join_backward.1 = (f32[24,128]{1,0:T(8,128)}, f32[2,2048]{1,0:T(2,128)}, f32[896,512]{1,0:T(8,128)}, f32[896,512]{1,0:T(8,128)}, bf16[4,512,128]{2,1,0:T(8,128)(2,1)}, /*index=5*/bf16[4,512,128]{2,1,0:T(8,128)(2,1)}) custom-call(s32[10]{0:T(128)} %pad_add_fusion.2.refs_0_, s32[2,32]{1,0:T(2,128)} %pad_add_fusion.refs_1_, bf16[32,1216,128]{2,1,0:T(8,128)(2,1)} %bitcast.196, ...), custom_call_target="tpu_custom_call" | custom-call | flops 20000000000 | bytes 30000000 | tf_op jit(solution)/shard_map/join_backward/pallas_call | solution.py:24
  244.4 15.0 %conv_backward.3 = (f32[896,512]{1,0:T(8,128)}, f32[2,128]{1,0:T(2,128)}, bf16[4,576,128]{2,1,0:T(8,128)(2,1)}, bf16[4,576,128]{2,1,0:T(8,128)(2,1)}) custom-call(s32[10]{0:T(128)} %pad_add_fusion.2.refs_0_, s32[2,40]{1,0:T(2,128)} %pad_add_fusion.1.refs_1_.refs_3_, bf16[4,832,128]{2,1,0:T(8,128)(2,1)} %pad_maximum_fusion.refs_2_.refs_4_, ...), custom_call_target="tpu_custom_call" | custom-call | flops 20000000000 | bytes 16000000 | tf_op jit(solution)/shard_map/conv_backward/pallas_call | solution.py:24
  260.8 13.9 %bottom_backward.1 = (bf16[896,512]{1,0:T(8,128)(2,1)}, bf16[4,336,128]{2,1,0:T(8,128)(2,1)}, bf16[4,336,128]{2,1,0:T(8,128)(2,1)}) custom-call(s32[10]{0:T(128)} %pad_add_fusion.2.refs_0_, s32[2,40]{1,0:T(2,128)} %pad_add_fusion.1.refs_1_.refs_3_, bf16[4,256,128]{2,1,0:T(8,128)(2,1)} %copy-done.5, bf16[4,256,128]{2,1,0:T(8,128)(2,1)} %collective-permute-done.15.refs_3_, ...), custom_call_target="tpu_custom_call" | custom-call | flops 10000000000 | bytes 16000000 | tf_op jit(solution)/shard_map/bottom_backward/pallas_call | solution.py:24
  274.7 1.5 collective-permute-start.26
  276.8 13.8 %collective-permute-done.42.refs_0_ = bf16[4,256,128]{2,1,0:T(8,128)(2,1)S(1)} collective-permute-done((bf16[4,256,128]{2,1,0:T(8,128)(2,1)S(1)}, bf16[4,256,128]{2,1,0:T(8,128)(2,1)S(1)}, u32[]{:S(2)}, u32[]{:S(2)}) %collective-permute-start.42) | collective-permute-done | bytes 262176 | tf_op jit(solution)/shard_map/ppermute | solution.py:969
  291.2 1.8 fold.9
  293.0 2.5 collective-permute-start.43
  295.5 2.0 collective-permute-start.45
  298.8 2.3 copy.113
  303.2 1.8 fold.5
  306.0 2.9 collective-permute-start.28
  309.8 1.7 collective-permute-done.27
  312.5 1.7 collective-permute-done.29
  319.6 2.0 fold.6
  321.6 2.1 collective-permute-start.31
  325.8 3.0 collective-permute-done.34.refs_0_
  329.6 2.1 fold.7
  332.6 6.5 %collective-permute-done.38.refs_0_ = bf16[4,592,128]{2,1,0:T(8,128)(2,1)S(1)} collective-permute-done((bf16[4,592,128]{2,1,0:T(8,128)(2,1)S(1)}, bf16[4,592,128]{2,1,0:T(8,128)(2,1)S(1)}, u32[]{:S(2)}, u32[]{:S(2)}) %collective-permute-start.38) | collective-permute-done | bytes 606240 | tf_op jit(solution)/shard_map/ppermute | solution.py:969
  340.0 2.1 fold.8
  342.9 2.5 collective-permute-start.37
  345.3 1.6 collective-permute-start.39
  346.9 2.8 collective-permute-start.40
  352.3 3.3 collective-permute-done.37
  355.6 1.6 collective-permute-done.39
  357.2 3.9 %collective-permute-done.40 = bf16[608,128]{1,0:T(8,128)(2,1)S(1)} collective-permute-done((bf16[608,128]{1,0:T(8,128)(2,1)}, bf16[608,128]{1,0:T(8,128)(2,1)S(1)}, u32[]{:S(2)}, u32[]{:S(2)}) %collective-permute-start.40) | collective-permute-done | bytes 155680 | tf_op jit(solution)/shard_map/ppermute | solution.py:972
  361.1 1.5 collective-permute-done.41
  (220 shorter events, 66.4 us)
Async XLA Ops:
  7.2 148.3 %all-gather.3.cloned.1.call-start = ((), (), s32[]{:S(2)}) async-start(), calls=%async_computation | async-start | bytes 10272768 | tf_op jit(solution)/shard_map/all_gather | solution.py:1088
  8.4 53.2 %copy-start = (bf16[1,16,7,7,2048]{4,1,3,2,0:T(8,128)(2,1)S(1)}, bf16[1,16,7,7,2048]{4,1,3,2,0:T(8,128)(2,1)}, u32[]{:S(2)}) copy-start(bf16[1,16,7,7,2048]{4,1,3,2,0:T(8,128)(2,1)} %param.16) | copy-start | bytes 9633796
  13.1 42.5 %collective-permute-start.14 = (bf16[256,128]{1,0:T(8,128)(2,1)S(1)}, bf16[256,128]{1,0:T(8,128)(2,1)S(1)}, u32[]{:S(2)}, u32[]{:S(2)}) collective-permute-start(bf16[256,128]{1,0:T(8,128)(2,1)S(1)} %bitcast.151), channel_id=1, source_target_pairs={{0,24},{4,28},{8,0},{12,4},{16,8},{20,12},{24,16},{28,20},{1,25},{... | collective-permute-start | bytes 196616 | tf_op jit(solution)/shard_map/ppermute | solution.py:972
  13.2 42.5 %collective-permute-start.13 = (bf16[256,128]{1,0:T(8,128)(2,1)S(1)}, bf16[256,128]{1,0:T(8,128)(2,1)}, u32[]{:S(2)}, u32[]{:S(2)}) collective-permute-start(bf16[256,128]{1,0:T(8,128)(2,1)S(1)} %bitcast.152), channel_id=1, source_target_pairs={{0,16},{4,20},{8,24},{12,28},{16,0},{20,4},{24,8},{28,12},{1,17},{... | collective-permute-start | bytes 196616 | tf_op jit(solution)/shard_map/ppermute | solution.py:972
  17.9 18.8 %collective-permute-start.1 = (bf16[832,128]{1,0:T(8,128)(2,1)}, bf16[832,128]{1,0:T(8,128)(2,1)}, u32[]{:S(2)}, u32[]{:S(2)}) collective-permute-start(bf16[832,128]{1,0:T(8,128)(2,1)} %get-tuple-element.162), channel_id=1, source_target_pairs={{0,16},{4,20},{8,24},{12,28},{16,0},{20,4},{24,8},{28,12},{1,17},{... | collective-permute-start | bytes 638984 | tf_op jit(solution)/shard_map/ppermute | solution.py:972
  17.9 27.9 %collective-permute-start = (bf16[832,128]{1,0:T(8,128)(2,1)}, bf16[832,128]{1,0:T(8,128)(2,1)}, u32[]{:S(2)}, u32[]{:S(2)}) collective-permute-start(bf16[832,128]{1,0:T(8,128)(2,1)} %get-tuple-element.162), channel_id=1, source_target_pairs={{0,8},{4,12},{8,16},{12,20},{16,24},{20,28},{24,0},{28,4},{1,9},{5... | collective-permute-start | bytes 638984 | tf_op jit(solution)/shard_map/ppermute | solution.py:972
  20.4 27.0 %collective-permute-start.2 = (bf16[832,128]{1,0:T(8,128)(2,1)}, bf16[832,128]{1,0:T(8,128)(2,1)}, u32[]{:S(2)}, u32[]{:S(2)}) collective-permute-start(bf16[832,128]{1,0:T(8,128)(2,1)} %get-tuple-element.162), channel_id=1, source_target_pairs={{0,24},{4,28},{8,0},{12,4},{16,8},{20,12},{24,16},{28,20},{1,25},{... | collective-permute-start | bytes 638984 | tf_op jit(solution)/shard_map/ppermute | solution.py:972
  36.7 19.0 %collective-permute-start.12 = (bf16[256,128]{1,0:T(8,128)(2,1)S(1)}, bf16[256,128]{1,0:T(8,128)(2,1)S(1)}, u32[]{:S(2)}, u32[]{:S(2)}) collective-permute-start(bf16[256,128]{1,0:T(8,128)(2,1)S(1)} %bitcast.153), channel_id=1, source_target_pairs={{0,8},{4,12},{8,16},{12,20},{16,24},{20,28},{24,0},{28,4},{1,9},{5... | collective-permute-start | bytes 196616 | tf_op jit(solution)/shard_map/ppermute | solution.py:972
  45.9 6.9 %collective-permute-start.24 = (f32[4,2,30,128]{3,1,2,0:T(2,128)S(1)}, f32[4,2,30,128]{3,1,2,0:T(2,128)}, u32[]{:S(2)}, u32[]{:S(2)}) collective-permute-start(f32[4,2,30,128]{3,1,2,0:T(2,128)S(1)} %bitcast_dynamic-update-slice_fusion), channel_id=1, source_target_pairs={{0,2},{1,3},{2,0},{3,1},{4,6},{5,7},{6,4},{7,5},{8,10},{9,11},{10,... | collective-permute-start | bytes 368648 | tf_op jit(solution)/shard_map/ppermute | solution.py:975
  49.5 32.3 %collective-permute-start.4 = (bf16[4,832,128]{2,1,0:T(8,128)(2,1)}, bf16[4,832,128]{2,1,0:T(8,128)(2,1)}, u32[]{:S(2)}, u32[]{:S(2)}) collective-permute-start(bf16[4,832,128]{2,1,0:T(8,128)(2,1)} %pad_maximum_fusion.refs_2_.refs_4_), channel_id=1, source_target_pairs={{0,2},{1,3},{2,0},{3,1},{4,6},{5,7},{6,4},{7,5},{8,10},{9,11},{10,... | collective-permute-start | bytes 2555912 | tf_op jit(solution)/shard_map/ppermute | solution.py:975
  52.8 35.6 %collective-permute-start.3 = (bf16[4,832,128]{2,1,0:T(8,128)(2,1)}, bf16[4,832,128]{2,1,0:T(8,128)(2,1)}, u32[]{:S(2)}, u32[]{:S(2)}) collective-permute-start(bf16[4,832,128]{2,1,0:T(8,128)(2,1)} %pad_maximum_fusion.refs_2_.refs_4_), channel_id=1, source_target_pairs={{0,4},{4,0},{8,12},{12,8},{16,20},{20,16},{24,28},{28,24},{1,5},{5... | collective-permute-start | bytes 2555912 | tf_op jit(solution)/shard_map/ppermute | solution.py:969
  55.7 11.3 %collective-permute-start.25 = (f32[4,2,30,128]{3,1,2,0:T(2,128)}, f32[4,2,30,128]{3,1,2,0:T(2,128)}, u32[]{:S(2)}, u32[]{:S(2)}) collective-permute-start(f32[4,2,30,128]{3,1,2,0:T(2,128)} %fusion.1), channel_id=1, source_target_pairs={{0,1},{1,0},{2,3},{3,2},{4,5},{5,4},{6,7},{7,6},{8,9},{9,8},{10,11... | collective-permute-start | bytes 368648 | tf_op jit(solution)/shard_map/ppermute | solution.py:978
  57.2 22.1 %collective-permute-start.16 = (bf16[4,256,128]{2,1,0:T(8,128)(2,1)S(1)}, bf16[4,256,128]{2,1,0:T(8,128)(2,1)}, u32[]{:S(2)}, u32[]{:S(2)}) collective-permute-start(bf16[4,256,128]{2,1,0:T(8,128)(2,1)S(1)} %pad_maximum_fusion.3.refs_2_), channel_id=1, source_target_pairs={{0,2},{1,3},{2,0},{3,1},{4,6},{5,7},{6,4},{7,5},{8,10},{9,11},{10,... | collective-permute-start | bytes 786440 | tf_op jit(solution)/shard_map/ppermute | solution.py:975
  58.5 28.4 %collective-permute-start.15 = (bf16[4,256,128]{2,1,0:T(8,128)(2,1)S(1)}, bf16[4,256,128]{2,1,0:T(8,128)(2,1)}, u32[]{:S(2)}, u32[]{:S(2)}) collective-permute-start(bf16[4,256,128]{2,1,0:T(8,128)(2,1)S(1)} %pad_maximum_fusion.3.refs_2_), channel_id=1, source_target_pairs={{0,4},{4,0},{8,12},{12,8},{16,20},{20,16},{24,28},{28,24},{1,5},{5... | collective-permute-start | bytes 786440 | tf_op jit(solution)/shard_map/ppermute | solution.py:969
  66.9 24.5 %collective-permute-start.19 = (bf16[4,256,128]{2,1,0:T(8,128)(2,1)S(1)}, bf16[4,256,128]{2,1,0:T(8,128)(2,1)S(1)}, u32[]{:S(2)}, u32[]{:S(2)}) collective-permute-start(bf16[4,256,128]{2,1,0:T(8,128)(2,1)S(1)} %pad_maximum_fusion.3.refs_2_), channel_id=1, source_target_pairs={{0,1},{1,0},{2,3},{3,2},{4,5},{5,4},{6,7},{7,6},{8,9},{9,8},{10,11... | collective-permute-start | bytes 786440 | tf_op jit(solution)/shard_map/ppermute | solution.py:978
  80.2 12.2 %collective-permute-start.18 = (bf16[4,128,128]{2,1,0:T(8,128)(2,1)S(1)}, bf16[4,128,128]{2,1,0:T(8,128)(2,1)S(1)}, u32[]{:S(2)}, u32[]{:S(2)}) collective-permute-start(bf16[4,128,128]{2,1,0:T(8,128)(2,1)S(1)} %slice.236), channel_id=1, source_target_pairs={{0,4},{4,0},{8,12},{12,8},{16,20},{20,16},{24,28},{28,24},{1,5},{5... | collective-permute-start | bytes 393224 | tf_op jit(solution)/shard_map/ppermute | solution.py:969
  81.8 15.1 %collective-permute-start.21 = (bf16[4,256,128]{2,1,0:T(8,128)(2,1)}, bf16[4,256,128]{2,1,0:T(8,128)(2,1)S(1)}, u32[]{:S(2)}, u32[]{:S(2)}) collective-permute-start(bf16[4,256,128]{2,1,0:T(8,128)(2,1)} %collective-permute-done.16.refs_4_), channel_id=1, source_target_pairs={{0,1},{1,0},{2,3},{3,2},{4,5},{5,4},{6,7},{7,6},{8,9},{9,8},{10,11... | collective-permute-start | bytes 786440 | tf_op jit(solution)/shard_map/ppermute | solution.py:978
  86.9 25.1 %collective-permute-start.6 = (bf16[4,448,128]{2,1,0:T(8,128)(2,1)S(1)}, bf16[4,448,128]{2,1,0:T(8,128)(2,1)}, u32[]{:S(2)}, u32[]{:S(2)}) collective-permute-start(bf16[4,448,128]{2,1,0:T(8,128)(2,1)S(1)} %slice.234), channel_id=1, source_target_pairs={{0,4},{4,0},{8,12},{12,8},{16,20},{20,16},{24,28},{28,24},{1,5},{5... | collective-permute-start | bytes 1376264 | tf_op jit(solution)/shard_map/ppermute | solution.py:969
  88.4 8.5 %collective-permute-start.17 = (bf16[4,128,128]{2,1,0:T(8,128)(2,1)S(1)}, bf16[4,128,128]{2,1,0:T(8,128)(2,1)S(1)}, u32[]{:S(2)}, u32[]{:S(2)}) collective-permute-start(bf16[4,128,128]{2,1,0:T(8,128)(2,1)S(1)} %slice.235), channel_id=1, source_target_pairs={{0,2},{1,3},{2,0},{3,1},{4,6},{5,7},{6,4},{7,5},{8,10},{9,11},{10,... | collective-permute-start | bytes 393224 | tf_op jit(solution)/shard_map/ppermute | solution.py:975
  91.4 6.6 %collective-permute-start.20 = (bf16[4,256,128]{2,1,0:T(8,128)(2,1)}, bf16[4,256,128]{2,1,0:T(8,128)(2,1)S(1)}, u32[]{:S(2)}, u32[]{:S(2)}) collective-permute-start(bf16[4,256,128]{2,1,0:T(8,128)(2,1)} %collective-permute-done.15.refs_3_), channel_id=1, source_target_pairs={{0,1},{1,0},{2,3},{3,2},{4,5},{5,4},{6,7},{7,6},{8,9},{9,8},{10,11... | collective-permute-start | bytes 786440 | tf_op jit(solution)/shard_map/ppermute | solution.py:978
  92.4 19.5 %collective-permute-start.5 = (bf16[4,384,128]{2,1,0:T(8,128)(2,1)S(1)}, bf16[4,384,128]{2,1,0:T(8,128)(2,1)}, u32[]{:S(2)}, u32[]{:S(2)}) collective-permute-start(bf16[4,384,128]{2,1,0:T(8,128)(2,1)S(1)} %slice.233), channel_id=1, source_target_pairs={{0,2},{1,3},{2,0},{3,1},{4,6},{5,7},{6,4},{7,5},{8,10},{9,11},{10,... | collective-permute-start | bytes 1179656 | tf_op jit(solution)/shard_map/ppermute | solution.py:975
  96.9 1.8 collective-permute-start.23
  96.9 1.9 collective-permute-start.22
  98.1 28.6 %collective-permute-start.7 = (bf16[4,832,128]{2,1,0:T(8,128)(2,1)}, bf16[4,832,128]{2,1,0:T(8,128)(2,1)S(1)}, u32[]{:S(2)}, u32[]{:S(2)}) collective-permute-start(bf16[4,832,128]{2,1,0:T(8,128)(2,1)} %pad_maximum_fusion.refs_2_.refs_4_), channel_id=1, source_target_pairs={{0,1},{1,0},{2,3},{3,2},{4,5},{5,4},{6,7},{7,6},{8,9},{9,8},{10,11... | collective-permute-start | bytes 2555912 | tf_op jit(solution)/shard_map/ppermute | solution.py:978
  98.7 28.0 %collective-permute-start.9 = (bf16[4,832,128]{2,1,0:T(8,128)(2,1)}, bf16[4,832,128]{2,1,0:T(8,128)(2,1)S(1)}, u32[]{:S(2)}, u32[]{:S(2)}) collective-permute-start(bf16[4,832,128]{2,1,0:T(8,128)(2,1)} %collective-permute-done.4.refs_4_.refs_6_), channel_id=1, source_target_pairs={{0,1},{1,0},{2,3},{3,2},{4,5},{5,4},{6,7},{7,6},{8,9},{9,8},{10,11... | collective-permute-start | bytes 2555912 | tf_op jit(solution)/shard_map/ppermute | solution.py:978
  98.9 27.9 %collective-permute-start.8 = (bf16[4,832,128]{2,1,0:T(8,128)(2,1)}, bf16[4,832,128]{2,1,0:T(8,128)(2,1)S(1)}, u32[]{:S(2)}, u32[]{:S(2)}) collective-permute-start(bf16[4,832,128]{2,1,0:T(8,128)(2,1)} %collective-permute-done.3.refs_3_.refs_5_), channel_id=1, source_target_pairs={{0,1},{1,0},{2,3},{3,2},{4,5},{5,4},{6,7},{7,6},{8,9},{9,8},{10,11... | collective-permute-start | bytes 2555912 | tf_op jit(solution)/shard_map/ppermute | solution.py:978
  111.9 14.8 %collective-permute-start.10 = (bf16[4,384,128]{2,1,0:T(8,128)(2,1)}, bf16[4,384,128]{2,1,0:T(8,128)(2,1)S(1)}, u32[]{:S(2)}, u32[]{:S(2)}) collective-permute-start(bf16[4,384,128]{2,1,0:T(8,128)(2,1)} %collective-permute-done.5.refs_5_.refs_7_), channel_id=1, source_target_pairs={{0,1},{1,0},{2,3},{3,2},{4,5},{5,4},{6,7},{7,6},{8,9},{9,8},{10,11... | collective-permute-start | bytes 1179656 | tf_op jit(solution)/shard_map/ppermute | solution.py:978
  111.9 14.8 %collective-permute-start.11 = (bf16[4,448,128]{2,1,0:T(8,128)(2,1)}, bf16[4,448,128]{2,1,0:T(8,128)(2,1)S(1)}, u32[]{:S(2)}, u32[]{:S(2)}) collective-permute-start(bf16[4,448,128]{2,1,0:T(8,128)(2,1)} %collective-permute-done.6.refs_6_.refs_8_), channel_id=1, source_target_pairs={{0,1},{1,0},{2,3},{3,2},{4,5},{5,4},{6,7},{7,6},{8,9},{9,8},{10,11... | collective-permute-start | bytes 1376264 | tf_op jit(solution)/shard_map/ppermute | solution.py:978
  274.7 27.8 %collective-permute-start.26 = (bf16[4,336,128]{2,1,0:T(8,128)(2,1)}, bf16[4,336,128]{2,1,0:T(8,128)(2,1)S(1)}, u32[]{:S(2)}, u32[]{:S(2)}) collective-permute-start(bf16[4,336,128]{2,1,0:T(8,128)(2,1)} %get-tuple-element.125), channel_id=1, source_target_pairs={{0,4},{4,0},{8,12},{12,8},{16,20},{20,16},{24,28},{28,24},{1,5},{5... | collective-permute-start | bytes 1032200 | tf_op jit(solution)/shard_map/ppermute | solution.py:969
  276.2 14.3 %collective-permute-start.42 = (bf16[4,256,128]{2,1,0:T(8,128)(2,1)S(1)}, bf16[4,256,128]{2,1,0:T(8,128)(2,1)S(1)}, u32[]{:S(2)}, u32[]{:S(2)}) collective-permute-start(bf16[4,256,128]{2,1,0:T(8,128)(2,1)S(1)} %copy-done.23), channel_id=1, source_target_pairs={{0,4},{4,0},{8,12},{12,8},{16,20},{20,16},{24,28},{28,24},{1,5},{5... | collective-permute-start | bytes 786440 | tf_op jit(solution)/shard_map/ppermute | solution.py:969
  293.0 12.1 %collective-permute-start.43 = (bf16[256,128]{1,0:T(8,128)(2,1)}, bf16[256,128]{1,0:T(8,128)(2,1)S(1)}, u32[]{:S(2)}, u32[]{:S(2)}) collective-permute-start(bf16[256,128]{1,0:T(8,128)(2,1)} %get-tuple-element.152), channel_id=1, source_target_pairs={{0,16},{4,20},{8,24},{12,28},{16,0},{20,4},{24,8},{28,12},{1,17},{... | collective-permute-start | bytes 196616 | tf_op jit(solution)/shard_map/ppermute | solution.py:972
  295.5 10.5 %collective-permute-start.44 = (bf16[256,128]{1,0:T(8,128)(2,1)}, bf16[256,128]{1,0:T(8,128)(2,1)S(1)}, u32[]{:S(2)}, u32[]{:S(2)}) collective-permute-start(bf16[256,128]{1,0:T(8,128)(2,1)} %get-tuple-element.153), channel_id=1, source_target_pairs={{0,8},{4,12},{8,16},{12,20},{16,24},{20,28},{24,0},{28,4},{1,9},{5... | collective-permute-start | bytes 196616 | tf_op jit(solution)/shard_map/ppermute | solution.py:972
  295.5 13.4 %collective-permute-start.45 = (bf16[256,128]{1,0:T(8,128)(2,1)}, bf16[256,128]{1,0:T(8,128)(2,1)S(1)}, u32[]{:S(2)}, u32[]{:S(2)}) collective-permute-start(bf16[256,128]{1,0:T(8,128)(2,1)} %get-tuple-element.154), channel_id=1, source_target_pairs={{0,24},{4,28},{8,0},{12,4},{16,8},{20,12},{24,16},{28,20},{1,25},{... | collective-permute-start | bytes 196616 | tf_op jit(solution)/shard_map/ppermute | solution.py:972
  301.1 17.7 %collective-permute-start.30 = (bf16[4,512,128]{2,1,0:T(8,128)(2,1)}, bf16[4,512,128]{2,1,0:T(8,128)(2,1)S(1)}, u32[]{:S(2)}, u32[]{:S(2)}) collective-permute-start(bf16[4,512,128]{2,1,0:T(8,128)(2,1)} %get-tuple-element.131), channel_id=1, source_target_pairs={{0,4},{4,0},{8,12},{12,8},{16,20},{20,16},{24,28},{28,24},{1,5},{5... | collective-permute-start | bytes 1572872 | tf_op jit(solution)/shard_map/ppermute | solution.py:969
  302.5 26.3 %collective-permute-start.34 = (bf16[4,576,128]{2,1,0:T(8,128)(2,1)S(1)}, bf16[4,576,128]{2,1,0:T(8,128)(2,1)S(1)}, u32[]{:S(2)}, u32[]{:S(2)}) collective-permute-start(bf16[4,576,128]{2,1,0:T(8,128)(2,1)S(1)} %copy-done.17), channel_id=1, source_target_pairs={{0,4},{4,0},{8,12},{12,8},{16,20},{20,16},{24,28},{28,24},{1,5},{5... | collective-permute-start | bytes 1769480 | tf_op jit(solution)/shard_map/ppermute | solution.py:969
  305.1 6.4 %collective-permute-start.27 = (bf16[336,128]{1,0:T(8,128)(2,1)}, bf16[336,128]{1,0:T(8,128)(2,1)S(1)}, u32[]{:S(2)}, u32[]{:S(2)}) collective-permute-start(bf16[336,128]{1,0:T(8,128)(2,1)} %get-tuple-element.128), channel_id=1, source_target_pairs={{0,16},{4,20},{8,24},{12,28},{16,0},{20,4},{24,8},{28,12},{1,17},{... | collective-permute-start | bytes 258056 | tf_op jit(solution)/shard_map/ppermute | solution.py:972
  306.0 6.5 %collective-permute-start.28 = (bf16[336,128]{1,0:T(8,128)(2,1)}, bf16[336,128]{1,0:T(8,128)(2,1)S(1)}, u32[]{:S(2)}, u32[]{:S(2)}) collective-permute-start(bf16[336,128]{1,0:T(8,128)(2,1)} %get-tuple-element.129), channel_id=1, source_target_pairs={{0,8},{4,12},{8,16},{12,20},{16,24},{20,28},{24,0},{28,4},{1,9},{5... | collective-permute-start | bytes 258056 | tf_op jit(solution)/shard_map/ppermute | solution.py:972
  308.9 5.3 %collective-permute-start.29 = (bf16[336,128]{1,0:T(8,128)(2,1)}, bf16[336,128]{1,0:T(8,128)(2,1)S(1)}, u32[]{:S(2)}, u32[]{:S(2)}) collective-permute-start(bf16[336,128]{1,0:T(8,128)(2,1)} %get-tuple-element.130), channel_id=1, source_target_pairs={{0,24},{4,28},{8,0},{12,4},{16,8},{20,12},{24,16},{28,20},{1,25},{... | collective-permute-start | bytes 258056 | tf_op jit(solution)/shard_map/ppermute | solution.py:972
  311.4 27.7 %collective-permute-start.38 = (bf16[4,592,128]{2,1,0:T(8,128)(2,1)S(1)}, bf16[4,592,128]{2,1,0:T(8,128)(2,1)S(1)}, u32[]{:S(2)}, u32[]{:S(2)}) collective-permute-start(bf16[4,592,128]{2,1,0:T(8,128)(2,1)S(1)} %copy-done.16), channel_id=1, source_target_pairs={{0,4},{4,0},{8,12},{12,8},{16,20},{20,16},{24,28},{28,24},{1,5},{5... | collective-permute-start | bytes 1818632 | tf_op jit(solution)/shard_map/ppermute | solution.py:969
  321.6 21.2 %collective-permute-start.31 = (bf16[512,128]{1,0:T(8,128)(2,1)}, bf16[512,128]{1,0:T(8,128)(2,1)S(1)}, u32[]{:S(2)}, u32[]{:S(2)}) collective-permute-start(bf16[512,128]{1,0:T(8,128)(2,1)} %get-tuple-element.134), channel_id=1, source_target_pairs={{0,16},{4,20},{8,24},{12,28},{16,0},{20,4},{24,8},{28,12},{1,17},{... | collective-permute-start | bytes 393224 | tf_op jit(solution)/shard_map/ppermute | solution.py:972
  323.8 21.6 %collective-permute-start.32 = (bf16[512,128]{1,0:T(8,128)(2,1)}, bf16[512,128]{1,0:T(8,128)(2,1)S(1)}, u32[]{:S(2)}, u32[]{:S(2)}) collective-permute-start(bf16[512,128]{1,0:T(8,128)(2,1)} %get-tuple-element.135), channel_id=1, source_target_pairs={{0,8},{4,12},{8,16},{12,20},{16,24},{20,28},{24,0},{28,4},{1,9},{5... | collective-permute-start | bytes 393224 | tf_op jit(solution)/shard_map/ppermute | solution.py:972
  324.8 22.1 %collective-permute-start.33 = (bf16[512,128]{1,0:T(8,128)(2,1)}, bf16[512,128]{1,0:T(8,128)(2,1)S(1)}, u32[]{:S(2)}, u32[]{:S(2)}) collective-permute-start(bf16[512,128]{1,0:T(8,128)(2,1)} %get-tuple-element.136), channel_id=1, source_target_pairs={{0,24},{4,28},{8,0},{12,4},{16,8},{20,12},{24,16},{28,20},{1,25},{... | collective-permute-start | bytes 393224 | tf_op jit(solution)/shard_map/ppermute | solution.py:972
  331.7 20.5 %collective-permute-start.35 = (bf16[576,128]{1,0:T(8,128)(2,1)}, bf16[576,128]{1,0:T(8,128)(2,1)S(1)}, u32[]{:S(2)}, u32[]{:S(2)}) collective-permute-start(bf16[576,128]{1,0:T(8,128)(2,1)} %get-tuple-element.140), channel_id=1, source_target_pairs={{0,16},{4,20},{8,24},{12,28},{16,0},{20,4},{24,8},{28,12},{1,17},{... | collective-permute-start | bytes 442376 | tf_op jit(solution)/shard_map/ppermute | solution.py:972
  339.1 13.1 %collective-permute-start.36 = (bf16[576,128]{1,0:T(8,128)(2,1)}, bf16[576,128]{1,0:T(8,128)(2,1)S(1)}, u32[]{:S(2)}, u32[]{:S(2)}) collective-permute-start(bf16[576,128]{1,0:T(8,128)(2,1)} %get-tuple-element.141), channel_id=1, source_target_pairs={{0,8},{4,12},{8,16},{12,20},{16,24},{20,28},{24,0},{28,4},{1,9},{5... | collective-permute-start | bytes 442376 | tf_op jit(solution)/shard_map/ppermute | solution.py:972
  342.9 12.7 %collective-permute-start.37 = (bf16[576,128]{1,0:T(8,128)(2,1)}, bf16[576,128]{1,0:T(8,128)(2,1)S(1)}, u32[]{:S(2)}, u32[]{:S(2)}) collective-permute-start(bf16[576,128]{1,0:T(8,128)(2,1)} %get-tuple-element.142), channel_id=1, source_target_pairs={{0,24},{4,28},{8,0},{12,4},{16,8},{20,12},{24,16},{28,20},{1,25},{... | collective-permute-start | bytes 442376 | tf_op jit(solution)/shard_map/ppermute | solution.py:972
  345.3 11.9 %collective-permute-start.39 = (bf16[608,128]{1,0:T(8,128)(2,1)}, bf16[608,128]{1,0:T(8,128)(2,1)S(1)}, u32[]{:S(2)}, u32[]{:S(2)}) collective-permute-start(bf16[608,128]{1,0:T(8,128)(2,1)} %get-tuple-element.146), channel_id=1, source_target_pairs={{0,16},{4,20},{8,24},{12,28},{16,0},{20,4},{24,8},{28,12},{1,17},{... | collective-permute-start | bytes 466952 | tf_op jit(solution)/shard_map/ppermute | solution.py:972
  346.9 14.2 %collective-permute-start.40 = (bf16[608,128]{1,0:T(8,128)(2,1)}, bf16[608,128]{1,0:T(8,128)(2,1)S(1)}, u32[]{:S(2)}, u32[]{:S(2)}) collective-permute-start(bf16[608,128]{1,0:T(8,128)(2,1)} %get-tuple-element.147), channel_id=1, source_target_pairs={{0,8},{4,12},{8,16},{12,20},{16,24},{20,28},{24,0},{28,4},{1,9},{5... | collective-permute-start | bytes 466952 | tf_op jit(solution)/shard_map/ppermute | solution.py:972
  352.2 10.4 %collective-permute-start.41 = (bf16[608,128]{1,0:T(8,128)(2,1)}, bf16[608,128]{1,0:T(8,128)(2,1)S(1)}, u32[]{:S(2)}, u32[]{:S(2)}) collective-permute-start(bf16[608,128]{1,0:T(8,128)(2,1)} %get-tuple-element.148), channel_id=1, source_target_pairs={{0,24},{4,28},{8,0},{12,4},{16,8},{20,12},{24,16},{28,20},{1,25},{... | collective-permute-start | bytes 466952 | tf_op jit(solution)/shard_map/ppermute | solution.py:972
  (27 other events, 278.0 us)
Sparse Core Ops, SparseCore 0:
  13.3 115.3 all-gather.2
